TPU v7x, 1024 devices: a whole 8x8x8 slice. The times are simulated.
1024 devices in a mesh: expert: 16 (over x, core), replica: 64 (over y, z).
Axes of the slice: x: 8, y: 8, z: 8, core: 2. Of those that a mesh axis runs over, the one named last changes fastest.
Arguments:
- grad_out: bfloat16 [131072, 3584], P(('expert', 'replica')), may hold values from -6 to 6
- route_probs: bfloat16 [131072, 1], P(('expert', 'replica')), may hold values from 0.099609375 to 1
- routes: int32 [131072, 1], P(('expert', 'replica')), may hold values from 0 to 15; in each aligned block of 128 rows (0 to 127, 128 to 255, ...) at most 12 rows name the same one
- hidden_saved: bfloat16 [16, 64, 16, 12, 1024], P('expert', 'replica'), may hold values from -6 to 6
- weight_codes: bfloat16 [16, 1024, 3584], P('expert'), may hold values from -6 to 6, as said below
- weight_scales: int32 [16, 1024, 112], P('expert'), may hold values from 118 to 121
- subset_ids: int32 [16, 384], P('expert'), may hold values from 0 to 1023, as said below
Outputs:
- hidden_grad: bfloat16 [16, 64, 16, 12, 1024], P('expert', 'replica')
- weight_grad: float32 [16, 3584, 384], P('expert', 'replica')
- prob_grad: float32 [131072, 1], P(('expert', 'replica'))
Inputs may be any that keep to these rules, and one draw needn't show every extreme that they name: Among the rows of one device no expert is named by more than 12 routes, and in some devices' rows an expert is named by exactly 12. `subset_ids`: each row holds 384 different hidden units. `weight_codes`: entries are of the four-bit code set: 0 and plus or minus 0.5, 1, 1.5, 2, 3, 4, 6.
All inputs are finite; a program needn't handle non-finite values.
Results may differ from a plain program's by a relative error of at most 0.0075.
Values may be sent and summed in bfloat16 or wider, within the bound.
No kernel may reach another device: no remote copies, remote signals or barrier semaphores. Data moves between devices by JAX's collectives and lax.ppermute only.
A program may use at most 64 MiB of HBM per device.

v0:
```python
import jax
import jax.numpy as jnp
from jax import lax
from jax.sharding import PartitionSpec as P


def per_device(
    grad_out, route_probs, routes, hidden_saved, weight_codes, weight_scales, subset_ids
):
    experts_n = lax.axis_size("expert")
    replicas = lax.axis_size("replica")
    width = grad_out.shape[1]
    hidden_n = weight_codes.shape[1]
    slots = hidden_saved.shape[3]
    repeats = routes.shape[1]
    flat_routes = routes.reshape(-1)
    onehot = (flat_routes[:, None] == jnp.arange(experts_n, dtype=jnp.int32)[None, :]).astype(
        jnp.int32
    )
    before = jnp.cumsum(onehot, axis=0) - onehot
    slot_index = jnp.sum(onehot * before, axis=1)
    target = flat_routes * slots + slot_index
    place_matrix = (
        target[:, None] == jnp.arange(experts_n * slots, dtype=jnp.int32)[None, :]
    ).astype(jnp.bfloat16)
    grad_rows = jnp.repeat(grad_out, repeats, axis=0)
    send_rows = lax.dot_general(
        place_matrix, grad_rows, (((0,), (0,)), ((), ())), preferred_element_type=jnp.float32
    )
    send_rows = send_rows.astype(jnp.bfloat16).reshape(experts_n, slots, width)
    send_probs = jnp.sum(
        place_matrix.astype(jnp.float32) * route_probs.reshape(-1).astype(jnp.float32)[:, None],
        axis=0,
    )
    send_probs = send_probs.astype(jnp.bfloat16).reshape(experts_n, slots)
    recv_rows, recv_probs = (
        lax.all_to_all(send_rows, "expert", split_axis=0, concat_axis=0, tiled=True),
        lax.all_to_all(send_probs, "expert", split_axis=0, concat_axis=0, tiled=True),
    )
    rows_recv = recv_rows.reshape(-1, width)
    weights_e = recv_probs.reshape(-1).astype(jnp.float32)
    scale_bf = jnp.exp2((weight_scales[0] - 127).astype(jnp.float32)).astype(jnp.bfloat16)
    weight = (weight_codes[0].reshape(hidden_n, width // 32, 32) * scale_bf[:, :, None]).reshape(
        hidden_n, width
    )
    hidden = hidden_saved.reshape(-1, hidden_n)
    picked = jnp.take(hidden, subset_ids[0], axis=1)
    scaled_hidden = (weights_e[:, None] * picked.astype(jnp.float32)).astype(jnp.bfloat16)
    weight_grad = lax.psum_scatter(
        lax.dot_general(
            rows_recv, scaled_hidden, (((0,), (0,)), ((), ())), preferred_element_type=jnp.float32
        ),
        "replica",
        scatter_dimension=0,
        tiled=True,
    )
    through = lax.dot_general(
        rows_recv, weight, (((1,), (1,)), ((), ())), preferred_element_type=jnp.float32
    )
    hidden_grad = (weights_e[:, None] * through).astype(jnp.bfloat16)
    expert_out = jnp.dot(hidden, weight, preferred_element_type=jnp.float32).astype(jnp.bfloat16)
    scores = jnp.sum(rows_recv.astype(jnp.float32) * expert_out.astype(jnp.float32), axis=1)
    returned = lax.all_to_all(
        scores.reshape(experts_n, slots), "expert", split_axis=0, concat_axis=0, tiled=True
    )
    prob_grad = jnp.take(returned.reshape(-1), target)
    return (
        hidden_grad.reshape(hidden_saved.shape),
        weight_grad.reshape(1, width // replicas, -1),
        prob_grad.reshape(routes.shape),
    )


def solution(mesh):
    placed = (
        P(("expert", "replica"), None),
        P(("expert", "replica"), None),
        P(("expert", "replica"), None),
        P("expert", "replica", None, None, None),
        P("expert", None, None),
        P("expert", None, None),
        P("expert", None),
    )
    return jax.shard_map(
        per_device,
        mesh=mesh,
        in_specs=placed,
        out_specs=(
            P("expert", "replica", None, None, None),
            P("expert", "replica", None),
            P(("expert", "replica"), None),
        ),
        check_vma=False,
    )
```

profile of v0, /device:TPU:6, one launch (start us, length us, event | category | flops | bytes accessed | tf_op | source)
XLA Modules:
  0.0 352.7 jit_solution(16197632518884611422)
XLA Ops:
  7.2 0.0 copy-start
  7.2 0.7 bitcast_convert_fusion
  7.9 0.7 fusion.32
  8.7 0.2 reduce_window_sum.11
  8.8 0.8 select_reduce_fusion
  9.7 0.7 fusion.36
  10.3 0.1 multiply_reduce_fusion
  10.4 0.7 convert_element_type.93
  11.2 16.4 %all-to-all-start = ((bf16[16,1,12]{2,1,0:T(2,128)(2,1)}), bf16[16,1,12]{2,1,0:T(2,128)(2,1)S(1)}, u32[]{:S(2)}, u32[]{:S(2)}) async-start(bf16[16,1,12]{2,1,0:T(2,128)(2,1)} %convert_element_type.93), calls=%async_computation | async-start | bytes 16384 | tf_op jit(solution)/shard_map/all_to_all | solution.py:38
  27.6 0.0 copy-done
  27.6 0.5 convolution_convert_fusion
  28.1 0.0 copy-start.4
  28.1 0.0 copy-start.2
  28.1 1.4 reshape.121
  29.5 2.5 all-to-all-done
  32.0 7.4 %all-to-all-start.1 = ((bf16[16,12,3584]{2,1,0:T(8,128)(2,1)}), bf16[16,12,3584]{2,1,0:T(8,128)(2,1)}, u32[]{:S(2)}, u32[]{:S(2)}) async-start(bf16[16,12,3584]{2,1,0:T(8,128)(2,1)} %reshape.121), calls=%async_computation.1 | async-start | bytes 3670016 | tf_op jit(solution)/shard_map/all_to_all | solution.py:37
  39.4 0.0 reduce-scatter.4.cloned.1.call-start
  39.4 0.0 copy-done.4
  39.4 0.0 copy-done.2
  39.5 0.2 copy.25
  39.7 0.1 reshape.124
  39.8 0.2 copy.26
  40.0 2.1 gather_fusion
  42.1 0.1 reshape.128
  42.2 40.3 %all-to-all-done.1 = bf16[16,12,3584]{2,1,0:T(8,128)(2,1)} async-done(((bf16[16,12,3584]{2,1,0:T(8,128)(2,1)}), bf16[16,12,3584]{2,1,0:T(8,128)(2,1)}, u32[]{:S(2)}, u32[]{:S(2)}) %all-to-all-start.1) | async-done | bytes 1376288 | tf_op jit(solution)/shard_map/all_to_all | solution.py:37
  82.6 2.4 reshape.122
  84.9 3.6 %fusion.26 = f32[3584,384]{1,0:T(8,128)} fusion(bf16[192,3584]{1,0:T(8,128)(2,1)S(1)} %reshape.122, f32[192]{0:T(256)S(1)} %reshape.128, bf16[384,192]{1,0:T(8,128)(2,1)S(1)} %gather_fusion, pred[384]{0:T(512)(128)(4,1)S(1)} %compare_and_fusion), kind=kOutput, calls=%fused_computation.18 | convolution fusion | flops 528777216 | bytes 7029888 | tf_op jit(solution)/shard_map/dot_general | solution.py:50
  88.6 0.0 reduce-scatter.4.cloned.1.call-update
  88.6 0.0 copy-start.1
  88.6 10.5 %copy.24 = bf16[1,1024,3584]{1,2,0:T(8,128)(2,1)} copy(bf16[1,1024,3584]{2,1,0:T(8,128)(2,1)} %param.11) | data formatting | bytes 14680064 | tf_op args[4]
  99.1 0.0 copy-done.1
  99.1 0.1 fusion.25
  99.2 6.6 %bitcast_multiply_fusion = bf16[1,1024,3584]{1,2,0:T(8,128)(2,1)} fusion(bf16[1,1024,3584]{1,2,0:T(8,128)(2,1)} %copy.24, bf16[1024,112]{0,1:T(8,128)(2,1)S(1)} %fusion.25), kind=kLoop, calls=%fused_computation.6 | loop fusion | flops 3670016 | bytes 14909440 | tf_op jit(solution)/shard_map/mul | solution.py:43
  105.8 5.8 %fusion.16 = f32[192]{0:T(256)S(1)} fusion(bf16[192,1024]{1,0:T(8,128)(2,1)S(1)} %reshape.124, bf16[1,1024,3584]{1,2,0:T(8,128)(2,1)} %bitcast_multiply_fusion, bf16[192,3584]{1,0:T(8,128)(2,1)S(1)} %reshape.122), kind=kOutput, calls=%fused_computation.12 | convolution fusion | flops 1412726528 | bytes 9110272 | tf_op jit(solution)/shard_map/dot_general | solution.py:61
  111.5 0.7 all_to_all.15
  112.2 5.3 %all-to-all-start.2 = ((f32[16,1,12]{2,1,0:T(1,128)}), f32[16,1,12]{2,1,0:T(1,128)S(1)}, u32[]{:S(2)}, u32[]{:S(2)}) async-start(f32[16,1,12]{2,1,0:T(1,128)} %bitcast.10), calls=%async_computation.2 | async-start | bytes 16384 | tf_op jit(solution)/shard_map/all_to_all | solution.py:63
  117.5 0.0 copy-start.3
  117.5 4.7 %fusion.22 = bf16[192,1024]{1,0:T(8,128)(2,1)S(1)} fusion(bf16[192,3584]{1,0:T(8,128)(2,1)S(1)} %reshape.122, bf16[1,1024,3584]{1,2,0:T(8,128)(2,1)} %bitcast_multiply_fusion, f32[192]{0:T(256)S(1)} %reshape.128), kind=kOutput, calls=%fused_computation.14 | convolution fusion | flops 1409679360 | bytes 9110272 | tf_op jit(solution)/shard_map/dot_general | solution.py:57
  122.2 0.1 reshape.123
  122.3 1.0 copy.28
  123.3 0.0 all-to-all-done.2
  123.3 0.5 broadcast.91
  123.8 0.7 reduce.10
  124.5 0.1 reshape.126
  124.6 1.3 gather_fusion.1
  125.8 0.0 copy-done.3
  125.9 0.5 and_select_fusion
  126.4 219.5 %reduce-scatter.4.cloned.1.call-done = f32[56,384]{1,0:T(8,128)} async-done(((f32[3584,384]{1,0:T(8,128)}), f32[56,384]{1,0:T(8,128)}) %reduce-scatter.4.cloned.1.call-update) | async-done | bytes 86032
  (6 shorter events, 0.1 us)
Async XLA Ops:
  7.2 20.4 %copy-start = (bf16[128,3584]{1,0:T(8,128)(2,1)S(1)}, bf16[128,3584]{1,0:T(8,128)(2,1)}, u32[]{:S(2)}) copy-start(bf16[128,3584]{1,0:T(8,128)(2,1)} %param.7) | copy-start | bytes 2752516
  11.2 20.8 %all-to-all-start = ((bf16[16,1,12]{2,1,0:T(2,128)(2,1)}), bf16[16,1,12]{2,1,0:T(2,128)(2,1)S(1)}, u32[]{:S(2)}, u32[]{:S(2)}) async-start(bf16[16,1,12]{2,1,0:T(2,128)(2,1)} %convert_element_type.93), calls=%async_computation | async-start | bytes 16384 | tf_op jit(solution)/shard_map/all_to_all | solution.py:38
  28.1 11.3 %copy-start.4 = (s32[1,384]{1,0:T(1,128)S(1)}, s32[1,384]{1,0:T(1,128)}, u32[]{:S(2)}) copy-start(s32[1,384]{1,0:T(1,128)} %param.13) | copy-start | bytes 4612
  28.1 11.3 %copy-start.2 = (bf16[1,1,16,12,1024]{4,2,3,1,0:T(8,128)(2,1)S(1)}, bf16[1,1,16,12,1024]{4,2,3,1,0:T(8,128)(2,1)}, u32[]{:S(2)}) copy-start(bf16[1,1,16,12,1024]{4,2,3,1,0:T(8,128)(2,1)} %param.10) | copy-start | bytes 1179652
  32.0 50.6 %all-to-all-start.1 = ((bf16[16,12,3584]{2,1,0:T(8,128)(2,1)}), bf16[16,12,3584]{2,1,0:T(8,128)(2,1)}, u32[]{:S(2)}, u32[]{:S(2)}) async-start(bf16[16,12,3584]{2,1,0:T(8,128)(2,1)} %reshape.121), calls=%async_computation.1 | async-start | bytes 3670016 | tf_op jit(solution)/shard_map/all_to_all | solution.py:37
  39.4 306.5 %reduce-scatter.4.cloned.1.call-start = ((), (), s32[]{:S(2)}) async-start(), calls=%async_computation.4 | async-start | bytes 5591040
  88.6 10.5 %copy-start.1 = (s32[1,1024,112]{1,2,0:T(8,128)S(1)}, s32[1,1024,112]{1,2,0:T(8,128)}, u32[]{:S(2)}) copy-start(s32[1,1024,112]{1,2,0:T(8,128)} %param.12) | copy-start | bytes 1376260
  112.2 11.1 %all-to-all-start.2 = ((f32[16,1,12]{2,1,0:T(1,128)}), f32[16,1,12]{2,1,0:T(1,128)S(1)}, u32[]{:S(2)}, u32[]{:S(2)}) async-start(f32[16,1,12]{2,1,0:T(1,128)} %bitcast.10), calls=%async_computation.2 | async-start | bytes 16384 | tf_op jit(solution)/shard_map/all_to_all | solution.py:63
  117.5 8.4 %copy-start.3 = (s32[128,1]{0,1:T(1,128)S(1)}, s32[128,1]{0,1:T(1,128)}, u32[]{:S(2)}) copy-start(s32[128,1]{0,1:T(1,128)} %param.9) | copy-start | bytes 1540
Sparse Core Ops, SparseCore 0:
  88.7 257.0 reduce-scatter.3
where the time goes:
time: 353 us
  waiting for transfers between devices  262 us (74%)
  starting transfers between devices  29.1 us (8%)
  local copies, waits for them, and re-layouts  21.2 us (6%)
  matrix products  14.6 us (4%)
  between operations  14.2 us (4%)
  other arithmetic  11.2 us (3%)
    unnamed x2, waiting for transfers between devices  219 us
    all_to_all x1, waiting for transfers between devices, per_device(): lax.all_to_all(send_rows, 'expert', split_axis=0, concat_axis=0, tiled=True)  40.3 us
    all_to_all x1, starting transfers between devices, per_device(): lax.all_to_all(send_probs, 'expert', split_axis=0, concat_axis=0, tiled=T...  16.4 us
    unnamed x13, local copies, waits for them, and re-layouts  11.7 us
    all_to_all x1, starting transfers between devices, per_device(): lax.all_to_all(send_rows, 'expert', split_axis=0, concat_axis=0, tiled=True)  7.39 us
  transfers between devices with their start and end apart: 4, of which 3 were waited for; matrix products, arithmetic and copies ran while one was open for 10% of the time, Pallas kernels for 0%

commit v1 on v0

v1 whole, which is shorter than its diff:
```python
import functools

import jax
import jax.numpy as jnp
from jax import lax
from jax.experimental import pallas as pl
from jax.experimental.pallas import tpu as pltpu
from jax.sharding import PartitionSpec as P

F32 = jnp.float32
BF16 = jnp.bfloat16
BOTH = ("expert", "replica")
LIMIT = 48 * 1024 * 1024


def iota(shape, dim):
    return lax.broadcasted_iota(jnp.int32, shape, dim)


def ones_where(mask):
    return jnp.where(mask, 1.0, 0.0).astype(BF16)


def contract(a, b, da, db):
    return lax.dot_general(a, b, (((da,), (db,)), ((), ())), preferred_element_type=F32)


def slots_of(routes_row, experts_n):
    rows = routes_row.shape[1]
    named = iota((experts_n, rows), 0) == routes_row
    earlier = ones_where(iota((rows, rows), 0) < iota((rows, rows), 1))
    before = contract(ones_where(named), earlier, 1, 0)
    return named, jnp.sum(jnp.where(named, before, 0.0), axis=0, keepdims=True).astype(jnp.int32)


def pack_kernel(slots, experts_n, routes_ref, probs_ref, grad_ref, out_ref):
    routes = routes_ref[...]
    probs = probs_ref[...].astype(F32)
    rows = routes.shape[1]
    half = out_ref.shape[1]
    _, slot = slots_of(routes, experts_n)
    target = routes * (2 * slots) + slot
    places = iota((out_ref.shape[0], rows), 0)
    left = jnp.where(places == target, probs, 0.0).astype(BF16)
    right = jnp.where(places == target + slots, probs, 0.0).astype(BF16)
    place = jnp.concatenate([left, right], axis=1)
    step = 256
    for at in range(0, half, step):
        piece = jnp.concatenate(
            [grad_ref[:, at : at + step], grad_ref[:, half + at : half + at + step]], axis=0
        )
        out_ref[:, at : at + step] = contract(place, piece, 1, 0).astype(BF16)


def pick_kernel(ids_ref, hidden_ref, out_ref):
    chosen = ones_where(iota((hidden_ref.shape[1], ids_ref.shape[1]), 0) == ids_ref[...])
    out_ref[...] = contract(hidden_ref[...], chosen, 1, 0).astype(BF16)


def relay_kernel(slots, sources, side, parity_ref, rows_ref, out_ref, total):
    half = rows_ref.shape[1]
    width = 2 * half
    piece = width // (side * side)
    main = side * piece
    rows = rows_ref.shape[0]
    lane = iota((rows, 256), 1)
    place = jnp.where(lane < 128, lane, 128 + (lane & 63))
    slot, source = place >> 4, place & 15
    step = half // 2
    for at in range(0, width, step):
        pick = ones_where(
            iota((rows, 256), 0) == source * (2 * slots) + (at // half) * slots + slot
        )
        block = rows_ref[:, at % half : at % half + step]
        total[at : at + step, :] = contract(block, pick, 0, 0)
    low = iota((piece, 128), 1) < 64

    def spread(where):
        for to in range(side):
            for part in range(side):
                at = where(to, part) * piece
                out_ref[to, part * piece : (part + 1) * piece, :] = total[
                    at : at + piece, 0:128
                ].astype(BF16)
            for part in range(side // 2):
                one = where(to, part) * piece
                two = where(to, part + side // 2) * piece
                both = jnp.where(
                    low, total[one : one + piece, 128:256], total[two : two + piece, 128:256]
                )
                out_ref[to, main + part * piece : main + (part + 1) * piece, :] = both.astype(BF16)

    @pl.when(parity_ref[0] == 0)
    def _():
        spread(lambda to, part: to * side + part)

    @pl.when(parity_ref[0] == 1)
    def _():
        spread(lambda to, part: part * side + to)


def hidden_kernel(
    slots, sources, rows_ref, codes_ref, scales_ref, hidden_ref, out_ref, score_ref, total, factors
):
    step_n = pl.program_id(0)
    block = codes_ref.shape[1]
    halves = pl.num_programs(0) // 2
    groups = scales_ref.shape[0]
    places = hidden_ref.shape[0]

    @pl.when(step_n == 0)
    def _():
        factors[...] = jnp.exp2((scales_ref[...] - 127).astype(F32)).T.astype(BF16)
        total[...] = jnp.zeros_like(total)

    at = step_n * (block // 32) + (iota((groups, block), 1) >> 5)
    spread = contract(factors[...], ones_where(iota((groups, block), 0) == at), 1, 0)
    weight = codes_ref[...] * spread.astype(BF16)
    place = iota((places, rows_ref.shape[0]), 0)
    row = (place & 15) * (2 * slots) + (step_n // halves) * slots + (place >> 4)
    pick = ones_where(iota((places, rows_ref.shape[0]), 1) == row)
    rows = contract(pick, rows_ref[...], 1, 0).astype(BF16)
    total[...] += contract(rows, weight, 1, 1)

    @pl.when(step_n == pl.num_programs(0) - 1)
    def _():
        through = total[...]
        out_ref[...] = through.astype(BF16)
        score = jnp.sum(through * hidden_ref[...].astype(F32), axis=1, keepdims=True)
        by_slot = jnp.where(iota((places, 128), 1) == iota((places, 128), 0) >> 4, score, 0.0)
        by_source = jnp.where(
            iota((sources, places), 0) == iota((sources, places), 1) & 15, 1.0, 0.0
        )
        score_ref[...] = jnp.dot(
            by_source, by_slot, preferred_element_type=F32, precision=lax.Precision.HIGHEST
        )


def partial_kernel(side, me_ref, relayed_ref, *refs):
    picked, out_ref, total = refs[:-2], refs[-2], refs[-1]
    main = out_ref.shape[0]
    half = main // 2
    zeros = jnp.zeros((64, out_ref.shape[1]), BF16)
    total[...] = jnp.zeros_like(total)
    for distance in range(side):
        block = relayed_ref.at[lax.rem(me_ref[0] - distance + side, side)]
        own = picked[distance]
        total[...] += contract(block[:main, :], own[0:128, :], 1, 0)
        rest = own[128:192, :]
        tail = block[main : main + half, :]
        total[:half, :] += contract(tail, jnp.concatenate([rest, zeros], axis=0), 1, 0)
        total[half:, :] += contract(tail, jnp.concatenate([zeros, rest], axis=0), 1, 0)
    out_ref[...] = total[...].astype(BF16)


def prob_kernel(experts_n, routes_ref, probs_ref, returned_ref, out_ref):
    routes = routes_ref[...]
    named, slot = slots_of(routes, experts_n)
    mine = lax.dot_general(
        returned_ref[...],
        jnp.where(named, 1.0, 0.0),
        (((0,), (0,)), ((), ())),
        preferred_element_type=F32,
        precision=lax.Precision.HIGHEST,
    )
    score = jnp.sum(jnp.where(iota(mine.shape, 0) == slot, mine, 0.0), axis=0, keepdims=True)
    out_ref[...] = score / probs_ref[...].astype(F32)


VMEM = pl.BlockSpec(memory_space=pltpu.VMEM)
SMEM = pl.BlockSpec(memory_space=pltpu.SMEM)


def cost(flops, moved):
    return pl.CostEstimate(flops=flops, bytes_accessed=moved, transcendentals=0)


def per_device(
    side, grad_out, route_probs, routes, hidden_saved, weight_codes, weight_scales, subset_ids
):
    experts_n = lax.axis_size("expert")
    width = grad_out.shape[1]
    sources, slots, hidden_n = hidden_saved.shape[2:]
    subset = subset_ids.shape[1]
    places = sources * slots
    half = width // 2
    main = width // side
    replica = lax.axis_index("replica")
    parity = lax.axis_index("expert") % 2
    me = jnp.where(parity == 0, replica // side, replica % side).astype(jnp.int32)
    params = pltpu.CompilerParams(vmem_limit_bytes=LIMIT)

    def at(e, y, z):
        return e * side * side + (y % side) * side + z % side

    lines = [
        [[at(e, b, a) if e % 2 == turn else at(e, a, b) for b in range(side)] for e in range(experts_n) for a in range(side)]
        for turn in (0, 1)
    ]

    def moves(by):
        return [
            (at(e, y, z), at(e, y + by, z) if e % 2 == 0 else at(e, y, z + by))
            for e in range(experts_n)
            for y in range(side)
            for z in range(side)
        ]

    def exchange(x, turn):
        return lax.all_to_all(
            x, BOTH, split_axis=0, concat_axis=0, tiled=True, axis_index_groups=lines[turn]
        )

    routes_row = routes.reshape(1, -1)
    probs_row = route_probs.reshape(1, -1)
    hidden = hidden_saved.transpose(0, 1, 3, 2, 4).reshape(places, hidden_n)

    packed = pl.pallas_call(
        functools.partial(pack_kernel, slots, experts_n),
        out_shape=jax.ShapeDtypeStruct((2 * places, half), BF16),
        in_specs=[VMEM] * 3,
        out_specs=VMEM,
        compiler_params=params,
        cost_estimate=cost(8 * places * 128 * half, 3 * places * width),
    )(routes_row, probs_row, grad_out)
    received = lax.all_to_all(
        packed.reshape(experts_n, 2 * slots, half), "expert", split_axis=0, concat_axis=0, tiled=True
    ).reshape(2 * places, half)

    ids, _ = lax.optimization_barrier((subset_ids, packed))
    picked = pl.pallas_call(
        pick_kernel,
        out_shape=jax.ShapeDtypeStruct((places, subset), BF16),
        in_specs=[VMEM] * 2,
        out_specs=VMEM,
        compiler_params=params,
        cost_estimate=cost(2 * places * hidden_n * subset, 2 * places * hidden_n),
    )(ids, hidden)
    others = [lax.ppermute(picked, BOTH, moves(by)) for by in range(1, side)]
    received, others = lax.optimization_barrier((received, others))

    relay = pl.pallas_call(
        functools.partial(relay_kernel, slots, sources, side),
        out_shape=jax.ShapeDtypeStruct((side, main + main // 2, 128), BF16),
        in_specs=[SMEM, VMEM],
        out_specs=VMEM,
        scratch_shapes=[pltpu.VMEM((width, 256), F32)],
        compiler_params=params,
        cost_estimate=cost(8 * places * 256 * half, 4 * places * width),
    )(parity.reshape(1), received)
    relayed = exchange(relay, 0)

    blocks = 4
    hidden_grad, scores = pl.pallas_call(
        functools.partial(hidden_kernel, slots, sources),
        grid=(blocks,),
        out_shape=(
            jax.ShapeDtypeStruct((places, hidden_n), BF16),
            jax.ShapeDtypeStruct((sources, 128), F32),
        ),
        in_specs=[
            pl.BlockSpec((2 * places, width // blocks), lambda i: (0, i % (blocks // 2))),
            pl.BlockSpec((hidden_n, width // blocks), lambda i: (0, i)),
            pl.BlockSpec((width // 32, hidden_n), lambda i: (0, 0)),
            pl.BlockSpec((places, hidden_n), lambda i: (0, 0)),
        ],
        out_specs=(
            pl.BlockSpec((places, hidden_n), lambda i: (0, 0)),
            pl.BlockSpec((sources, 128), lambda i: (0, 0)),
        ),
        scratch_shapes=[
            pltpu.VMEM((places, hidden_n), F32),
            pltpu.VMEM((hidden_n, width // 32), BF16),
        ],
        compiler_params=params,
        cost_estimate=cost(4 * places * hidden_n * width, 2 * hidden_n * width),
    )(received, weight_codes[0], weight_scales[0].T, hidden)
    returned = lax.all_to_all(scores, "expert", split_axis=0, concat_axis=0, tiled=True)

    summed = pl.pallas_call(
        functools.partial(partial_kernel, side),
        out_shape=jax.ShapeDtypeStruct((main, subset), BF16),
        in_specs=[SMEM] + [VMEM] * (side + 1),
        out_specs=VMEM,
        scratch_shapes=[pltpu.VMEM((main, subset), F32)],
        compiler_params=params,
        cost_estimate=cost(2 * side * places * main * subset, 2 * side * places * (main + subset)),
    )(me.reshape(1), relayed, picked, *others)
    terms = exchange(summed.reshape(side, main // side, subset), 1)
    weight_grad = jnp.sum(terms.astype(F32), axis=0)

    prob_grad = pl.pallas_call(
        functools.partial(prob_kernel, experts_n),
        out_shape=jax.ShapeDtypeStruct(routes_row.shape, F32),
        in_specs=[VMEM] * 3,
        out_specs=VMEM,
        compiler_params=params,
    )(routes_row, probs_row, returned)
    return (
        hidden_grad.reshape(1, 1, slots, sources, hidden_n).transpose(0, 1, 3, 2, 4),
        weight_grad.reshape(1, main // side, subset),
        prob_grad.reshape(routes.shape),
    )


def solution(mesh):
    side = 8
    placed = (
        P(("expert", "replica"), None),
        P(("expert", "replica"), None),
        P(("expert", "replica"), None),
        P("expert", "replica", None, None, None),
        P("expert", None, None),
        P("expert", None, None),
        P("expert", None),
    )
    return jax.shard_map(
        functools.partial(per_device, side),
        mesh=mesh,
        in_specs=placed,
        out_specs=(
            P("expert", "replica", None, None, None),
            P("expert", "replica", None),
            P(("expert", "replica"), None),
        ),
        check_vma=False,
    )
```

time: 353 us -> 121 us (0.34)
  the two profiles are of different devices: /device:TPU:6 before, /device:TPU:2 now
where the time goes in v1:
time: 121 us; the launch traced here: 120 us
  starting transfers between devices  63 us (52%)
  waiting for transfers between devices  31.9 us (26%)
  Pallas kernels  15.4 us (13%)
  local copies, waits for them, and re-layouts  8.34 us (7%)
    ppermute x7, starting transfers between devices, per_device(): others = [lax.ppermute(picked, BOTH, moves(by)) for by in range(1, side)]  23.4 us
    all_to_all x2, waiting for transfers between devices, exchange(): lax.all_to_all(x, BOTH, split_axis=0, concat_axis=0, tiled=True, axis_ind...  22.2 us
    all_to_all x1, starting transfers between devices, per_device(): lax.all_to_all(packed.reshape(experts_n, 2 * slots, half), 'expert', spli...  16.8 us
    all_to_all x2, starting transfers between devices, exchange(): lax.all_to_all(x, BOTH, split_axis=0, concat_axis=0, tiled=True, axis_ind...  14 us
    all_to_all x1, starting transfers between devices, per_device(): lax.all_to_all(scores, 'expert', split_axis=0, concat_axis=0, tiled=True)  8.91 us
    pallas_call x1, Pallas kernels, per_device(): pl.pallas_call(functools.partial(hidden_kernel, slots, sources), grid=(bl...  8.8 us
    ppermute x7, waiting for transfers between devices, per_device(): others = [lax.ppermute(picked, BOTH, moves(by)) for by in range(1, side)]  8.66 us
    unnamed x32, local copies, waits for them, and re-layouts  8.34 us
  transfers between devices with their start and end apart: 11, of which 5 were waited for; matrix products, arithmetic and copies ran while one was open for 0% of the time, Pallas kernels for 10%

profile of v1, /device:TPU:2, one launch (start us, length us, event | category | flops | bytes accessed | tf_op | source)
XLA Modules:
  0.0 120.2 jit_solution(10144559181564416576)
XLA Ops:
  0.6 0.0 copy-start.1
  0.6 1.2 copy-done.1
  1.8 0.0 copy-start.8
  1.8 0.7 copy-done.8
  2.5 0.7 copy-done.10
  3.1 1.8 %shard_map.94 = bf16[384,1792]{1,0:T(8,128)(2,1)} custom-call(s32[1,128]{1,0:T(1,128)S(1)} %bitcast.26, bf16[1,128]{1,0:T(2,128)(2,1)S(1)} %bitcast.28, bf16[128,3584]{1,0:T(8,128)(2,1)S(1)} %copy-done.1), custom_call_target="tpu_custom_call" | custom-call | flops 352321536 | bytes 2064384 | tf_op jit(solution)/shard_map/pallas_call | solution.py:218
  4.9 16.8 %all-to-all-start = ((bf16[16,24,1792]{2,1,0:T(8,128)(2,1)}), bf16[16,24,1792]{2,1,0:T(8,128)(2,1)S(1)}, u32[]{:S(2)}, u32[]{:S(2)}) async-start(bf16[16,24,1792]{2,1,0:T(8,128)(2,1)} %bitcast.2), calls=%async_computation | async-start | bytes 2752512 | tf_op jit(solution)/shard_map/all_to_all | solution.py:226
  21.7 0.0 copy-done.13
  21.7 0.0 copy-done.15
  21.7 0.4 shard_map.95.refs_0_
  22.1 1.9 %collective-permute-start.6 = (bf16[192,384]{1,0:T(8,128)(2,1)S(1)}, bf16[192,384]{1,0:T(8,128)(2,1)S(1)}, u32[]{:S(2)}, u32[]{:S(2)}) collective-permute-start(bf16[192,384]{1,0:T(8,128)(2,1)S(1)} %shard_map.95.refs_0_), channel_id=1, source_target_pairs={{0,56},{1,57},{2,58},{3,59},{4,60},{5,61},{6,62},{7,63},{8,0},{9,1... | collective-permute-start | bytes 442376 | tf_op jit(solution)/shard_map/ppermute | solution.py:239
  24.0 1.9 %collective-permute-start.5 = (bf16[192,384]{1,0:T(8,128)(2,1)S(1)}, bf16[192,384]{1,0:T(8,128)(2,1)S(1)}, u32[]{:S(2)}, u32[]{:S(2)}) collective-permute-start(bf16[192,384]{1,0:T(8,128)(2,1)S(1)} %shard_map.95.refs_0_), channel_id=1, source_target_pairs={{0,48},{1,49},{2,50},{3,51},{4,52},{5,53},{6,54},{7,55},{8,56},{9,... | collective-permute-start | bytes 442376 | tf_op jit(solution)/shard_map/ppermute | solution.py:239
  25.9 1.9 %collective-permute-start.4 = (bf16[192,384]{1,0:T(8,128)(2,1)S(1)}, bf16[192,384]{1,0:T(8,128)(2,1)S(1)}, u32[]{:S(2)}, u32[]{:S(2)}) collective-permute-start(bf16[192,384]{1,0:T(8,128)(2,1)S(1)} %shard_map.95.refs_0_), channel_id=1, source_target_pairs={{0,40},{1,41},{2,42},{3,43},{4,44},{5,45},{6,46},{7,47},{8,48},{9,... | collective-permute-start | bytes 442376 | tf_op jit(solution)/shard_map/ppermute | solution.py:239
  27.9 8.4 %collective-permute-start.3 = (bf16[192,384]{1,0:T(8,128)(2,1)S(1)}, bf16[192,384]{1,0:T(8,128)(2,1)S(1)}, u32[]{:S(2)}, u32[]{:S(2)}) collective-permute-start(bf16[192,384]{1,0:T(8,128)(2,1)S(1)} %shard_map.95.refs_0_), channel_id=1, source_target_pairs={{0,32},{1,33},{2,34},{3,35},{4,36},{5,37},{6,38},{7,39},{8,40},{9,... | collective-permute-start | bytes 442376 | tf_op jit(solution)/shard_map/ppermute | solution.py:239
  36.3 1.9 %collective-permute-start.2 = (bf16[192,384]{1,0:T(8,128)(2,1)S(1)}, bf16[192,384]{1,0:T(8,128)(2,1)S(1)}, u32[]{:S(2)}, u32[]{:S(2)}) collective-permute-start(bf16[192,384]{1,0:T(8,128)(2,1)S(1)} %shard_map.95.refs_0_), channel_id=1, source_target_pairs={{0,24},{1,25},{2,26},{3,27},{4,28},{5,29},{6,30},{7,31},{8,32},{9,... | collective-permute-start | bytes 442376 | tf_op jit(solution)/shard_map/ppermute | solution.py:239
  38.2 0.0 collective-permute-done.6.refs_7_
  38.2 4.8 %collective-permute-start.1 = (bf16[192,384]{1,0:T(8,128)(2,1)S(1)}, bf16[192,384]{1,0:T(8,128)(2,1)S(1)}, u32[]{:S(2)}, u32[]{:S(2)}) collective-permute-start(bf16[192,384]{1,0:T(8,128)(2,1)S(1)} %shard_map.95.refs_0_), channel_id=1, source_target_pairs={{0,16},{1,17},{2,18},{3,19},{4,20},{5,21},{6,22},{7,23},{8,24},{9,... | collective-permute-start | bytes 442376 | tf_op jit(solution)/shard_map/ppermute | solution.py:239
  43.0 0.0 collective-permute-done.5.refs_6_
  43.0 2.5 %collective-permute-start = (bf16[192,384]{1,0:T(8,128)(2,1)S(1)}, bf16[192,384]{1,0:T(8,128)(2,1)S(1)}, u32[]{:S(2)}, u32[]{:S(2)}) collective-permute-start(bf16[192,384]{1,0:T(8,128)(2,1)S(1)} %shard_map.95.refs_0_), channel_id=1, source_target_pairs={{0,8},{1,9},{2,10},{3,11},{4,12},{5,13},{6,14},{7,15},{8,16},{9,17... | collective-permute-start | bytes 442376 | tf_op jit(solution)/shard_map/ppermute | solution.py:239
  45.5 0.0 collective-permute-done.4.refs_5_
  45.5 0.0 collective-permute-done.3.refs_4_
  45.6 5.5 %collective-permute-done.2.refs_3_ = bf16[192,384]{1,0:T(8,128)(2,1)S(1)} collective-permute-done((bf16[192,384]{1,0:T(8,128)(2,1)S(1)}, bf16[192,384]{1,0:T(8,128)(2,1)S(1)}, u32[]{:S(2)}, u32[]{:S(2)}) %collective-permute-start.2) | collective-permute-done | bytes 147488 | tf_op jit(solution)/shard_map/ppermute | solution.py:239
  51.0 0.0 collective-permute-done.1.refs_2_
  51.0 3.2 %collective-permute-done.refs_1_ = bf16[192,384]{1,0:T(8,128)(2,1)S(1)} collective-permute-done((bf16[192,384]{1,0:T(8,128)(2,1)S(1)}, bf16[192,384]{1,0:T(8,128)(2,1)S(1)}, u32[]{:S(2)}, u32[]{:S(2)}) %collective-permute-start) | collective-permute-done | bytes 147488 | tf_op jit(solution)/shard_map/ppermute | solution.py:239
  54.2 0.0 all-to-all-done
  54.2 1.4 %shard_map.97 = bf16[8,672,128]{2,1,0:T(8,128)(2,1)S(1)} custom-call(s32[1]{0:T(128)} %bitcast.12.parity_ref, bf16[384,1792]{1,0:T(8,128)(2,1)S(1)} %bitcast.23), custom_call_target="tpu_custom_call" | custom-call | flops 704643072 | bytes 2752512 | tf_op jit(solution)/shard_map/pallas_call | solution.py:242
  55.6 0.0 copy-done.2
  55.6 0.0 copy-done.4
  55.6 0.0 copy-done.6
  55.6 0.0 copy-start
  55.6 1.1 copy-done
  56.7 4.1 %all-to-all-start.1 = ((bf16[8,672,128]{2,1,0:T(8,128)(2,1)}), bf16[8,672,128]{2,1,0:T(8,128)(2,1)S(1)}, u32[]{:S(2)}, u32[]{:S(2)}) async-start(bf16[8,672,128]{2,1,0:T(8,128)(2,1)} %copy-done), calls=%async_computation.1 | async-start | bytes 2752512 | tf_op jit(solution)/shard_map/all_to_all | solution.py:210
  60.8 1.0 copy-done.12
  61.8 1.0 copy-done.14
  62.8 8.8 %shard_map.96 = (bf16[192,1024]{1,0:T(8,128)(2,1)}, f32[16,128]{1,0:T(8,128)}) custom-call(bf16[384,1792]{1,0:T(8,128)(2,1)S(1)} %bitcast.24, bf16[1024,3584]{1,0:T(8,128)(2,1)} %bitcast.35, s32[112,1024]{1,0:T(8,128)S(1)} %bitcast.30, bf16[192,1024]{1,0:T(8,128)(2,1)S(1)} %bitcast.32), custom_call_target="tpu_custom_call" | custom-call | flops 2818572288 | bytes 7340032 | tf_op jit(solution)/shard_map/pallas_call | solution.py:254
  71.6 11.7 %all-to-all-done.1.relayed_ref = bf16[8,672,128]{2,1,0:T(8,128)(2,1)S(1)} async-done(((bf16[8,672,128]{2,1,0:T(8,128)(2,1)}), bf16[8,672,128]{2,1,0:T(8,128)(2,1)S(1)}, u32[]{:S(2)}, u32[]{:S(2)}) %all-to-all-start.1) | async-done | bytes 1376288 | tf_op jit(solution)/shard_map/all_to_all | solution.py:210
  83.3 8.9 %all-to-all-start.3 = ((f32[16,1,128]{2,1,0:T(1,128)}), f32[16,1,128]{2,1,0:T(1,128)S(1)}, u32[]{:S(2)}, u32[]{:S(2)}) async-start(f32[16,1,128]{2,1,0:T(1,128)} %bitcast.16), calls=%async_computation.3 | async-start | bytes 16384 | tf_op jit(solution)/shard_map/all_to_all | solution.py:278
  92.2 0.9 copy-done.3
  93.1 0.9 copy-done.5
  94.0 0.9 copy-done.7
  94.9 2.3 %shard_map.98 = bf16[448,384]{1,0:T(8,128)(2,1)} custom-call(s32[1]{0:T(128)} %bitcast.11.me_ref, bf16[8,672,128]{2,1,0:T(8,128)(2,1)S(1)} %all-to-all-done.1.relayed_ref, bf16[192,384]{1,0:T(8,128)(2,1)S(1)} %shard_map.95.refs_0_, bf16[192,384]{1,0:T(8,128)(2,1)S(1)} %copy-done.7, bf16[192,384]{1,0:T(8,128)(2,1)S(1)} %copy-done.5, ...), custom_call_target="tpu_custom_call" | custom-call | flops 528482304 | bytes 2555904 | tf_op jit(solution)/shard_map/pallas_call | solution.py:280
  97.2 1.1 all-to-all-done.3
  98.3 9.9 %all-to-all-start.2 = ((bf16[8,56,384]{2,1,0:T(8,128)(2,1)}), bf16[8,56,384]{2,1,0:T(8,128)(2,1)S(1)}, u32[]{:S(2)}, u32[]{:S(2)}) async-start(bf16[8,56,384]{2,1,0:T(8,128)(2,1)} %bitcast.13), calls=%async_computation.2 | async-start | bytes 688128 | tf_op jit(solution)/shard_map/all_to_all | solution.py:210
  108.2 0.0 copy-done.9
  108.2 0.0 copy-done.11
  108.2 0.8 shard_map.99
  109.0 10.6 %all-to-all-done.2 = bf16[8,56,384]{2,1,0:T(8,128)(2,1)S(1)} async-done(((bf16[8,56,384]{2,1,0:T(8,128)(2,1)}), bf16[8,56,384]{2,1,0:T(8,128)(2,1)S(1)}, u32[]{:S(2)}, u32[]{:S(2)}) %all-to-all-start.2) | async-done | bytes 344096 | tf_op jit(solution)/shard_map/all_to_all | solution.py:210
  119.5 0.7 convert_reduce_fusion
  (13 shorter events, 0.0 us)
Async XLA Ops:
  0.6 1.2 copy-start.1
  1.8 0.7 copy-start.8
  2.5 0.7 copy-start.10
  4.9 16.8 %copy-start.13 = (bf16[1,1,16,12,1024]{4,2,3,1,0:T(8,128)(2,1)S(1)}, bf16[1,1,16,12,1024]{4,2,3,1,0:T(8,128)(2,1)}, u32[]{:S(2)}) copy-start(bf16[1,1,16,12,1024]{4,2,3,1,0:T(8,128)(2,1)} %param.10) | copy-start | bytes 1179652
  4.9 16.8 %copy-start.15 = (s32[1,384]{1,0:T(1,128)S(1)}, s32[1,384]{1,0:T(1,128)}, u32[]{:S(2)}) copy-start(s32[1,384]{1,0:T(1,128)} %ids_ref) | copy-start | bytes 4612
  4.9 49.3 %all-to-all-start = ((bf16[16,24,1792]{2,1,0:T(8,128)(2,1)}), bf16[16,24,1792]{2,1,0:T(8,128)(2,1)S(1)}, u32[]{:S(2)}, u32[]{:S(2)}) async-start(bf16[16,24,1792]{2,1,0:T(8,128)(2,1)} %bitcast.2), calls=%async_computation | async-start | bytes 2752512 | tf_op jit(solution)/shard_map/all_to_all | solution.py:226
  22.1 16.1 %collective-permute-start.6 = (bf16[192,384]{1,0:T(8,128)(2,1)S(1)}, bf16[192,384]{1,0:T(8,128)(2,1)S(1)}, u32[]{:S(2)}, u32[]{:S(2)}) collective-permute-start(bf16[192,384]{1,0:T(8,128)(2,1)S(1)} %shard_map.95.refs_0_), channel_id=1, source_target_pairs={{0,56},{1,57},{2,58},{3,59},{4,60},{5,61},{6,62},{7,63},{8,0},{9,1... | collective-permute-start | bytes 442376 | tf_op jit(solution)/shard_map/ppermute | solution.py:239
  24.0 19.0 %collective-permute-start.5 = (bf16[192,384]{1,0:T(8,128)(2,1)S(1)}, bf16[192,384]{1,0:T(8,128)(2,1)S(1)}, u32[]{:S(2)}, u32[]{:S(2)}) collective-permute-start(bf16[192,384]{1,0:T(8,128)(2,1)S(1)} %shard_map.95.refs_0_), channel_id=1, source_target_pairs={{0,48},{1,49},{2,50},{3,51},{4,52},{5,53},{6,54},{7,55},{8,56},{9,... | collective-permute-start | bytes 442376 | tf_op jit(solution)/shard_map/ppermute | solution.py:239
  25.9 19.6 %collective-permute-start.4 = (bf16[192,384]{1,0:T(8,128)(2,1)S(1)}, bf16[192,384]{1,0:T(8,128)(2,1)S(1)}, u32[]{:S(2)}, u32[]{:S(2)}) collective-permute-start(bf16[192,384]{1,0:T(8,128)(2,1)S(1)} %shard_map.95.refs_0_), channel_id=1, source_target_pairs={{0,40},{1,41},{2,42},{3,43},{4,44},{5,45},{6,46},{7,47},{8,48},{9,... | collective-permute-start | bytes 442376 | tf_op jit(solution)/shard_map/ppermute | solution.py:239
  27.9 17.7 %collective-permute-start.3 = (bf16[192,384]{1,0:T(8,128)(2,1)S(1)}, bf16[192,384]{1,0:T(8,128)(2,1)S(1)}, u32[]{:S(2)}, u32[]{:S(2)}) collective-permute-start(bf16[192,384]{1,0:T(8,128)(2,1)S(1)} %shard_map.95.refs_0_), channel_id=1, source_target_pairs={{0,32},{1,33},{2,34},{3,35},{4,36},{5,37},{6,38},{7,39},{8,40},{9,... | collective-permute-start | bytes 442376 | tf_op jit(solution)/shard_map/ppermute | solution.py:239
  36.3 14.7 %collective-permute-start.2 = (bf16[192,384]{1,0:T(8,128)(2,1)S(1)}, bf16[192,384]{1,0:T(8,128)(2,1)S(1)}, u32[]{:S(2)}, u32[]{:S(2)}) collective-permute-start(bf16[192,384]{1,0:T(8,128)(2,1)S(1)} %shard_map.95.refs_0_), channel_id=1, source_target_pairs={{0,24},{1,25},{2,26},{3,27},{4,28},{5,29},{6,30},{7,31},{8,32},{9,... | collective-permute-start | bytes 442376 | tf_op jit(solution)/shard_map/ppermute | solution.py:239
  38.2 12.8 %collective-permute-start.1 = (bf16[192,384]{1,0:T(8,128)(2,1)S(1)}, bf16[192,384]{1,0:T(8,128)(2,1)S(1)}, u32[]{:S(2)}, u32[]{:S(2)}) collective-permute-start(bf16[192,384]{1,0:T(8,128)(2,1)S(1)} %shard_map.95.refs_0_), channel_id=1, source_target_pairs={{0,16},{1,17},{2,18},{3,19},{4,20},{5,21},{6,22},{7,23},{8,24},{9,... | collective-permute-start | bytes 442376 | tf_op jit(solution)/shard_map/ppermute | solution.py:239
  43.0 11.2 %collective-permute-start = (bf16[192,384]{1,0:T(8,128)(2,1)S(1)}, bf16[192,384]{1,0:T(8,128)(2,1)S(1)}, u32[]{:S(2)}, u32[]{:S(2)}) collective-permute-start(bf16[192,384]{1,0:T(8,128)(2,1)S(1)} %shard_map.95.refs_0_), channel_id=1, source_target_pairs={{0,8},{1,9},{2,10},{3,11},{4,12},{5,13},{6,14},{7,15},{8,16},{9,17... | collective-permute-start | bytes 442376 | tf_op jit(solution)/shard_map/ppermute | solution.py:239
  51.0 4.6 %copy-start.2 = (bf16[192,384]{1,0:T(8,128)(2,1)}, bf16[192,384]{1,0:T(8,128)(2,1)S(1)}, u32[]{:S(2)}) copy-start(bf16[192,384]{1,0:T(8,128)(2,1)S(1)} %collective-permute-done.2.refs_3_) | copy-start | bytes 442372
  51.0 4.6 %copy-start.4 = (bf16[192,384]{1,0:T(8,128)(2,1)}, bf16[192,384]{1,0:T(8,128)(2,1)S(1)}, u32[]{:S(2)}) copy-start(bf16[192,384]{1,0:T(8,128)(2,1)S(1)} %collective-permute-done.1.refs_2_) | copy-start | bytes 442372
  54.2 1.4 %copy-start.6 = (bf16[192,384]{1,0:T(8,128)(2,1)}, bf16[192,384]{1,0:T(8,128)(2,1)S(1)}, u32[]{:S(2)}) copy-start(bf16[192,384]{1,0:T(8,128)(2,1)S(1)} %collective-permute-done.refs_1_) | copy-start | bytes 442372
  55.6 1.1 copy-start
  56.7 26.5 %all-to-all-start.1 = ((bf16[8,672,128]{2,1,0:T(8,128)(2,1)}), bf16[8,672,128]{2,1,0:T(8,128)(2,1)S(1)}, u32[]{:S(2)}, u32[]{:S(2)}) async-start(bf16[8,672,128]{2,1,0:T(8,128)(2,1)} %copy-done), calls=%async_computation.1 | async-start | bytes 2752512 | tf_op jit(solution)/shard_map/all_to_all | solution.py:210
  60.8 1.0 copy-start.12
  61.8 1.0 copy-start.14
  83.3 15.0 %all-to-all-start.3 = ((f32[16,1,128]{2,1,0:T(1,128)}), f32[16,1,128]{2,1,0:T(1,128)S(1)}, u32[]{:S(2)}, u32[]{:S(2)}) async-start(f32[16,1,128]{2,1,0:T(1,128)} %bitcast.16), calls=%async_computation.3 | async-start | bytes 16384 | tf_op jit(solution)/shard_map/all_to_all | solution.py:278
  92.2 0.9 copy-start.3
  93.1 0.9 copy-start.5
  94.0 0.9 copy-start.7
  94.9 13.3 %copy-start.9 = (s32[128,1]{0,1:T(1,128)S(1)}, s32[128,1]{0,1:T(1,128)}, u32[]{:S(2)}) copy-start(s32[128,1]{0,1:T(1,128)} %param.9) | copy-start | bytes 1540
  94.9 13.3 %copy-start.11 = (bf16[128,1]{0,1:T(2,128)(2,1)S(1)}, bf16[128,1]{0,1:T(2,128)(2,1)}, u32[]{:S(2)}) copy-start(bf16[128,1]{0,1:T(2,128)(2,1)} %param.8) | copy-start | bytes 772
  98.3 21.2 %all-to-all-start.2 = ((bf16[8,56,384]{2,1,0:T(8,128)(2,1)}), bf16[8,56,384]{2,1,0:T(8,128)(2,1)S(1)}, u32[]{:S(2)}, u32[]{:S(2)}) async-start(bf16[8,56,384]{2,1,0:T(8,128)(2,1)} %bitcast.13), calls=%async_computation.2 | async-start | bytes 688128 | tf_op jit(solution)/shard_map/all_to_all | solution.py:210

commit v2 on v1

--- a/solution.py
+++ b/solution.py
@@ -10,7 +10,7 @@
 F32 = jnp.float32
 BF16 = jnp.bfloat16
 BOTH = ("expert", "replica")
-LIMIT = 48 * 1024 * 1024
+MIB = 1024 * 1024
 
 
 def iota(shape, dim):
@@ -33,23 +33,17 @@
     return named, jnp.sum(jnp.where(named, before, 0.0), axis=0, keepdims=True).astype(jnp.int32)
 
 
-def pack_kernel(slots, experts_n, routes_ref, probs_ref, grad_ref, out_ref):
+def pack_kernel(slots, experts_n, routes_ref, probs_ref, left_ref, right_ref, out_ref):
     routes = routes_ref[...]
     probs = probs_ref[...].astype(F32)
-    rows = routes.shape[1]
-    half = out_ref.shape[1]
     _, slot = slots_of(routes, experts_n)
     target = routes * (2 * slots) + slot
-    places = iota((out_ref.shape[0], rows), 0)
+    places = iota((out_ref.shape[0], routes.shape[1]), 0)
     left = jnp.where(places == target, probs, 0.0).astype(BF16)
     right = jnp.where(places == target + slots, probs, 0.0).astype(BF16)
     place = jnp.concatenate([left, right], axis=1)
-    step = 256
-    for at in range(0, half, step):
-        piece = jnp.concatenate(
-            [grad_ref[:, at : at + step], grad_ref[:, half + at : half + at + step]], axis=0
-        )
-        out_ref[:, at : at + step] = contract(place, piece, 1, 0).astype(BF16)
+    both = jnp.concatenate([left_ref[...], right_ref[...]], axis=0)
+    out_ref[...] = contract(place, both, 1, 0).astype(BF16)
 
 
 def pick_kernel(ids_ref, hidden_ref, out_ref):
@@ -99,38 +93,55 @@
         spread(lambda to, part: part * side + to)
 
 
-def hidden_kernel(
-    slots, sources, rows_ref, codes_ref, scales_ref, hidden_ref, out_ref, score_ref, total, factors
-):
+def weight_kernel(codes_ref, scales_ref, out_ref, factors):
+    block = codes_ref.shape[1]
+    groups = scales_ref.shape[0]
     step_n = pl.program_id(0)
-    block = codes_ref.shape[1]
-    halves = pl.num_programs(0) // 2
-    groups = scales_ref.shape[0]
-    places = hidden_ref.shape[0]
 
     @pl.when(step_n == 0)
     def _():
         factors[...] = jnp.exp2((scales_ref[...] - 127).astype(F32)).T.astype(BF16)
-        total[...] = jnp.zeros_like(total)
 
     at = step_n * (block // 32) + (iota((groups, block), 1) >> 5)
     spread = contract(factors[...], ones_where(iota((groups, block), 0) == at), 1, 0)
-    weight = codes_ref[...] * spread.astype(BF16)
+    out_ref[...] = codes_ref[...] * spread.astype(BF16)
+
+
+def hidden_kernel(slots, sources, me_ref, rows_hbm, weight_hbm, hidden_hbm, out_ref, *refs):
+    score_refs, (rows_ref, weight_ref, hidden_ref, rows, sems) = refs[:-5], refs[-5:]
+    radix = len(score_refs)
+    places, hidden_n = out_ref.shape
+    half = rows_ref.shape[1]
+    blocks = sems.shape[0] - 2
+    block = hidden_n // blocks
+    loads = [pltpu.make_async_copy(rows_hbm, rows_ref, sems.at[blocks])]
+    for n in range(blocks):
+        part = pl.ds(n * block, block)
+        loads.append(pltpu.make_async_copy(weight_hbm.at[part], weight_ref.at[part], sems.at[n]))
+    loads.insert(2, pltpu.make_async_copy(hidden_hbm, hidden_ref, sems.at[blocks + 1]))
+    for load in loads:
+        load.start()
+    rows_load, first_load, hidden_load, *rest = loads
     place = iota((places, rows_ref.shape[0]), 0)
-    row = (place & 15) * (2 * slots) + (step_n // halves) * slots + (place >> 4)
-    pick = ones_where(iota((places, rows_ref.shape[0]), 1) == row)
-    rows = contract(pick, rows_ref[...], 1, 0).astype(BF16)
-    total[...] += contract(rows, weight, 1, 1)
-
-    @pl.when(step_n == pl.num_programs(0) - 1)
-    def _():
-        through = total[...]
-        out_ref[...] = through.astype(BF16)
-        score = jnp.sum(through * hidden_ref[...].astype(F32), axis=1, keepdims=True)
-        by_slot = jnp.where(iota((places, 128), 1) == iota((places, 128), 0) >> 4, score, 0.0)
-        by_source = jnp.where(
-            iota((sources, places), 0) == iota((sources, places), 1) & 15, 1.0, 0.0
-        )
+    column = iota((places, rows_ref.shape[0]), 1)
+    rows_load.wait()
+    for part in range(2):
+        pick = ones_where(column == (place & 15) * (2 * slots) + part * slots + (place >> 4))
+        rows[:, part * half : (part + 1) * half] = contract(pick, rows_ref[...], 1, 0).astype(BF16)
+    hidden_load.wait()
+    score = jnp.zeros((places, 1), F32)
+    for n, load in enumerate([first_load, *rest]):
+        load.wait()
+        part = slice(n * block, (n + 1) * block)
+        through = contract(rows[...], weight_ref[part, :], 1, 1)
+        out_ref[:, part] = through.astype(BF16)
+        score += jnp.sum(through * hidden_ref[:, part].astype(F32), axis=1, keepdims=True)
+    by_slot = jnp.where(iota((places, 128), 1) == iota((places, 128), 0) >> 4, score, 0.0)
+    rows_n = sources // radix
+    ahead = iota((rows_n, places), 0) * radix + me_ref[0]
+    for low, score_ref in enumerate(score_refs):
+        to = (ahead + low) & 15
+        by_source = jnp.where(to == iota((rows_n, places), 1) & 15, 1.0, 0.0)
         score_ref[...] = jnp.dot(
             by_source, by_slot, preferred_element_type=F32, precision=lax.Precision.HIGHEST
         )
@@ -153,12 +164,29 @@
     out_ref[...] = total[...].astype(BF16)
 
 
-def prob_kernel(experts_n, routes_ref, probs_ref, returned_ref, out_ref):
+def with_bit(count, bit, value):
+    return [j for j in range(count) if (j >> bit) & 1 == value]
+
+
+def regroup_kernel(bit, *refs):
+    count = 2 * refs[0].shape[0]
+    for value in range(2):
+        rows = []
+        for j in with_bit(count, bit + 1, value):
+            held = (j >> bit) & 1
+            row = with_bit(count, bit, held).index(j)
+            rows.append(refs[held][row : row + 1, :])
+        refs[2 + value][...] = jnp.concatenate(rows, axis=0)
+
+
+def prob_kernel(experts_n, me_ref, routes_ref, probs_ref, *refs):
+    returned_refs, out_ref = refs[:-1], refs[-1]
     routes = routes_ref[...]
-    named, slot = slots_of(routes, experts_n)
+    _, slot = slots_of(routes, experts_n)
+    named = (me_ref[0] - iota((experts_n, routes.shape[1]), 0)) & (experts_n - 1)
     mine = lax.dot_general(
-        returned_ref[...],
-        jnp.where(named, 1.0, 0.0),
+        jnp.concatenate([ref[...] for ref in returned_refs], axis=0),
+        jnp.where(named == routes, 1.0, 0.0),
         (((0,), (0,)), ((), ())),
         preferred_element_type=F32,
         precision=lax.Precision.HIGHEST,
@@ -169,6 +197,7 @@
 
 VMEM = pl.BlockSpec(memory_space=pltpu.VMEM)
 SMEM = pl.BlockSpec(memory_space=pltpu.SMEM)
+HBM = pl.BlockSpec(memory_space=pltpu.HBM)
 
 
 def cost(flops, moved):
@@ -186,9 +215,12 @@
     half = width // 2
     main = width // side
     replica = lax.axis_index("replica")
+    expert = lax.axis_index("expert").reshape(1)
     parity = lax.axis_index("expert") % 2
+    radix = 2
     me = jnp.where(parity == 0, replica // side, replica % side).astype(jnp.int32)
-    params = pltpu.CompilerParams(vmem_limit_bytes=LIMIT)
+    params = pltpu.CompilerParams(vmem_limit_bytes=16 * MIB)
+    streamed = pltpu.CompilerParams(vmem_limit_bytes=56 * MIB)
 
     def at(e, y, z):
         return e * side * side + (y % side) * side + z % side
@@ -211,23 +243,34 @@
             x, BOTH, split_axis=0, concat_axis=0, tiled=True, axis_index_groups=lines[turn]
         )
 
+    def shifted(x, by):
+        return lax.ppermute(x, "expert", [(e, (e + by) % experts_n) for e in range(experts_n)])
+
     routes_row = routes.reshape(1, -1)
     probs_row = route_probs.reshape(1, -1)
     hidden = hidden_saved.transpose(0, 1, 3, 2, 4).reshape(places, hidden_n)
 
+    chunks = 2
+    tokens = grad_out.shape[0]
     packed = pl.pallas_call(
         functools.partial(pack_kernel, slots, experts_n),
+        grid=(chunks,),
         out_shape=jax.ShapeDtypeStruct((2 * places, half), BF16),
-        in_specs=[VMEM] * 3,
-        out_specs=VMEM,
-        compiler_params=params,
+        in_specs=[
+            pl.BlockSpec((1, tokens), lambda i: (0, 0)),
+            pl.BlockSpec((1, tokens), lambda i: (0, 0)),
+            pl.BlockSpec((tokens, half // chunks), lambda i: (0, i)),
+            pl.BlockSpec((tokens, half // chunks), lambda i: (0, i + chunks)),
+        ],
+        out_specs=pl.BlockSpec((2 * places, half // chunks), lambda i: (0, i)),
+        compiler_params=pltpu.CompilerParams(vmem_limit_bytes=63 * MIB),
         cost_estimate=cost(8 * places * 128 * half, 3 * places * width),
-    )(routes_row, probs_row, grad_out)
+    )(routes_row, probs_row, grad_out, grad_out)
     received = lax.all_to_all(
         packed.reshape(experts_n, 2 * slots, half), "expert", split_axis=0, concat_axis=0, tiled=True
     ).reshape(2 * places, half)
 
-    ids, _ = lax.optimization_barrier((subset_ids, packed))
+    ids, scales, _ = lax.optimization_barrier((subset_ids, weight_scales[0].T, packed))
     picked = pl.pallas_call(
         pick_kernel,
         out_shape=jax.ShapeDtypeStruct((places, subset), BF16),
@@ -237,7 +280,21 @@
         cost_estimate=cost(2 * places * hidden_n * subset, 2 * places * hidden_n),
     )(ids, hidden)
     others = [lax.ppermute(picked, BOTH, moves(by)) for by in range(1, side)]
-    received, others = lax.optimization_barrier((received, others))
+    blocks = 4
+    weight = pl.pallas_call(
+        weight_kernel,
+        grid=(blocks,),
+        out_shape=jax.ShapeDtypeStruct((hidden_n, width), BF16),
+        in_specs=[
+            pl.BlockSpec((hidden_n, width // blocks), lambda i: (0, i)),
+            pl.BlockSpec((width // 32, hidden_n), lambda i: (0, 0)),
+        ],
+        out_specs=pl.BlockSpec((hidden_n, width // blocks), lambda i: (0, i)),
+        scratch_shapes=[pltpu.VMEM((hidden_n, width // 32), BF16)],
+        compiler_params=streamed,
+        cost_estimate=cost(256 * hidden_n * width, 4 * hidden_n * width),
+    )(weight_codes[0], scales)
+    received, others, weight = lax.optimization_barrier((received, others, weight))
 
     relay = pl.pallas_call(
         functools.partial(relay_kernel, slots, sources, side),
@@ -250,33 +307,41 @@
     )(parity.reshape(1), received)
     relayed = exchange(relay, 0)
 
-    blocks = 4
-    hidden_grad, scores = pl.pallas_call(
+    hidden_grad, *scores = pl.pallas_call(
         functools.partial(hidden_kernel, slots, sources),
-        grid=(blocks,),
         out_shape=(
             jax.ShapeDtypeStruct((places, hidden_n), BF16),
-            jax.ShapeDtypeStruct((sources, 128), F32),
+            *[jax.ShapeDtypeStruct((sources // radix, 128), F32)] * radix,
         ),
-        in_specs=[
-            pl.BlockSpec((2 * places, width // blocks), lambda i: (0, i % (blocks // 2))),
-            pl.BlockSpec((hidden_n, width // blocks), lambda i: (0, i)),
-            pl.BlockSpec((width // 32, hidden_n), lambda i: (0, 0)),
-            pl.BlockSpec((places, hidden_n), lambda i: (0, 0)),
+        in_specs=[SMEM, HBM, HBM, HBM],
+        out_specs=(VMEM,) + (VMEM,) * radix,
+        scratch_shapes=[
+            pltpu.VMEM((2 * places, half), BF16),
+            pltpu.VMEM((hidden_n, width), BF16),
+            pltpu.VMEM((places, hidden_n), BF16),
+            pltpu.VMEM((places, width), BF16),
+            pltpu.SemaphoreType.DMA((2 + 2,)),
         ],
-        out_specs=(
-            pl.BlockSpec((places, hidden_n), lambda i: (0, 0)),
-            pl.BlockSpec((sources, 128), lambda i: (0, 0)),
-        ),
-        scratch_shapes=[
-            pltpu.VMEM((places, hidden_n), F32),
-            pltpu.VMEM((hidden_n, width // 32), BF16),
-        ],
-        compiler_params=params,
+        compiler_params=streamed,
         cost_estimate=cost(4 * places * hidden_n * width, 2 * hidden_n * width),
-    )(received, weight_codes[0], weight_scales[0].T, hidden)
-    returned = lax.all_to_all(scores, "expert", split_axis=0, concat_axis=0, tiled=True)
-
+    )(expert, received, weight, hidden)
+
+    def passed_on(bit, scores):
+        return [scores[0], shifted(scores[1], 1 << bit)]
+
+    def regrouped(bit, scores):
+        return pl.pallas_call(
+            functools.partial(regroup_kernel, bit),
+            out_shape=[jax.ShapeDtypeStruct((sources // radix, 128), F32)] * 2,
+            in_specs=[VMEM] * 2,
+            out_specs=[VMEM] * 2,
+            compiler_params=params,
+        )(*scores)
+
+    scores = regrouped(0, passed_on(0, scores))
+    scores = regrouped(1, passed_on(1, scores))
+    relayed, scores = lax.optimization_barrier((relayed, scores))
+    scores = passed_on(2, scores)
     summed = pl.pallas_call(
         functools.partial(partial_kernel, side),
         out_shape=jax.ShapeDtypeStruct((main, subset), BF16),
@@ -286,16 +351,18 @@
         compiler_params=params,
         cost_estimate=cost(2 * side * places * main * subset, 2 * side * places * (main + subset)),
     )(me.reshape(1), relayed, picked, *others)
+    summed, scores = lax.optimization_barrier((summed, scores))
+    returned = passed_on(3, regrouped(2, scores))
     terms = exchange(summed.reshape(side, main // side, subset), 1)
     weight_grad = jnp.sum(terms.astype(F32), axis=0)
 
     prob_grad = pl.pallas_call(
         functools.partial(prob_kernel, experts_n),
         out_shape=jax.ShapeDtypeStruct(routes_row.shape, F32),
-        in_specs=[VMEM] * 3,
+        in_specs=[SMEM] + [VMEM] * (2 + radix),
         out_specs=VMEM,
         compiler_params=params,
-    )(routes_row, probs_row, returned)
+    )(expert, routes_row, probs_row, *returned)
     return (
         hidden_grad.reshape(1, 1, slots, sources, hidden_n).transpose(0, 1, 3, 2, 4),
         weight_grad.reshape(1, main // side, subset),

time: 121 us -> 116 us (0.959)
  the two profiles are of different devices: /device:TPU:2 before, /device:TPU:4 now
where the time goes in v2:
time: 116 us; the launch traced here: 115 us
  starting transfers between devices  72.4 us (62%)
  Pallas kernels  23.1 us (20%)
  waiting for transfers between devices  17.6 us (15%)
    ppermute x7, starting transfers between devices, per_device(): others = [lax.ppermute(picked, BOTH, moves(by)) for by in range(1, side)]  24.6 us
    all_to_all x2, starting transfers between devices, exchange(): lax.all_to_all(x, BOTH, split_axis=0, concat_axis=0, tiled=True, axis_ind...  17 us
    all_to_all x1, starting transfers between devices, per_device(): lax.all_to_all(packed.reshape(experts_n, 2 * slots, half), 'expert', spli...  16.8 us
    ppermute x4, starting transfers between devices, shifted(): lax.ppermute(x, 'expert', [(e, (e + by) % experts_n) for e in range(exper...  14 us
    ppermute x4, waiting for transfers between devices, shifted(): lax.ppermute(x, 'expert', [(e, (e + by) % experts_n) for e in range(exper...  9.66 us
    all_to_all x2, waiting for transfers between devices, exchange(): lax.all_to_all(x, BOTH, split_axis=0, concat_axis=0, tiled=True, axis_ind...  7.89 us
    pallas_call x1, Pallas kernels, per_device(): pl.pallas_call(weight_kernel, grid=(blocks,), out_shape=jax.ShapeDtypeStr...  7.73 us
    pallas_call x1, Pallas kernels, per_device(): pl.pallas_call(functools.partial(hidden_kernel, slots, sources), out_shap...  6.25 us
  transfers between devices with their start and end apart: 14, of which 5 were waited for; matrix products, arithmetic and copies ran while one was open for 0% of the time, Pallas kernels for 15%

profile of v2, /device:TPU:4, one launch (start us, length us, event | category | flops | bytes accessed | tf_op | source)
XLA Modules:
  0.0 115.2 jit_solution(5886754513836176889)
XLA Ops:
  0.6 3.0 %shard_map.94 = bf16[384,1792]{1,0:T(8,128)(2,1)} custom-call(s32[1,128]{1,0:T(1,128)} %bitcast.22, bf16[1,128]{1,0:T(2,128)(2,1)} %bitcast.24, bf16[128,3584]{1,0:T(8,128)(2,1)} %right_ref.1, bf16[128,3584]{1,0:T(8,128)(2,1)} %right_ref.1), custom_call_target="tpu_custom_call" | custom-call | flops 352321536 | bytes 2064384 | tf_op jit(solution)/shard_map/pallas_call | solution.py:255
  3.7 0.0 copy-start.4
  3.7 0.0 copy-start.5
  3.7 16.8 %all-to-all-start = ((bf16[16,24,1792]{2,1,0:T(8,128)(2,1)}), bf16[16,24,1792]{2,1,0:T(8,128)(2,1)S(1)}, u32[]{:S(2)}, u32[]{:S(2)}) async-start(bf16[16,24,1792]{2,1,0:T(8,128)(2,1)} %bitcast.29), calls=%async_computation | async-start | bytes 2752512 | tf_op jit(solution)/shard_map/all_to_all | solution.py:269
  20.5 0.0 copy-done.4
  20.5 0.0 copy-done.5
  20.5 0.4 shard_map.95.refs_0_
  20.9 1.9 %collective-permute-start = (bf16[192,384]{1,0:T(8,128)(2,1)S(1)}, bf16[192,384]{1,0:T(8,128)(2,1)S(1)}, u32[]{:S(2)}, u32[]{:S(2)}) collective-permute-start(bf16[192,384]{1,0:T(8,128)(2,1)S(1)} %shard_map.95.refs_0_), channel_id=1, source_target_pairs={{0,8},{1,9},{2,10},{3,11},{4,12},{5,13},{6,14},{7,15},{8,16},{9,17... | collective-permute-start | bytes 442376 | tf_op jit(solution)/shard_map/ppermute | solution.py:282
  22.8 1.9 %collective-permute-start.1 = (bf16[192,384]{1,0:T(8,128)(2,1)S(1)}, bf16[192,384]{1,0:T(8,128)(2,1)S(1)}, u32[]{:S(2)}, u32[]{:S(2)}) collective-permute-start(bf16[192,384]{1,0:T(8,128)(2,1)S(1)} %shard_map.95.refs_0_), channel_id=1, source_target_pairs={{0,16},{1,17},{2,18},{3,19},{4,20},{5,21},{6,22},{7,23},{8,24},{9,... | collective-permute-start | bytes 442376 | tf_op jit(solution)/shard_map/ppermute | solution.py:282
  24.7 1.9 %collective-permute-start.2 = (bf16[192,384]{1,0:T(8,128)(2,1)S(1)}, bf16[192,384]{1,0:T(8,128)(2,1)S(1)}, u32[]{:S(2)}, u32[]{:S(2)}) collective-permute-start(bf16[192,384]{1,0:T(8,128)(2,1)S(1)} %shard_map.95.refs_0_), channel_id=1, source_target_pairs={{0,24},{1,25},{2,26},{3,27},{4,28},{5,29},{6,30},{7,31},{8,32},{9,... | collective-permute-start | bytes 442376 | tf_op jit(solution)/shard_map/ppermute | solution.py:282
  26.6 8.4 %collective-permute-start.3 = (bf16[192,384]{1,0:T(8,128)(2,1)S(1)}, bf16[192,384]{1,0:T(8,128)(2,1)S(1)}, u32[]{:S(2)}, u32[]{:S(2)}) collective-permute-start(bf16[192,384]{1,0:T(8,128)(2,1)S(1)} %shard_map.95.refs_0_), channel_id=1, source_target_pairs={{0,32},{1,33},{2,34},{3,35},{4,36},{5,37},{6,38},{7,39},{8,40},{9,... | collective-permute-start | bytes 442376 | tf_op jit(solution)/shard_map/ppermute | solution.py:282
  35.0 1.9 %collective-permute-start.4 = (bf16[192,384]{1,0:T(8,128)(2,1)S(1)}, bf16[192,384]{1,0:T(8,128)(2,1)S(1)}, u32[]{:S(2)}, u32[]{:S(2)}) collective-permute-start(bf16[192,384]{1,0:T(8,128)(2,1)S(1)} %shard_map.95.refs_0_), channel_id=1, source_target_pairs={{0,40},{1,41},{2,42},{3,43},{4,44},{5,45},{6,46},{7,47},{8,48},{9,... | collective-permute-start | bytes 442376 | tf_op jit(solution)/shard_map/ppermute | solution.py:282
  37.0 0.0 collective-permute-done.refs_1_
  37.0 6.0 %collective-permute-start.5 = (bf16[192,384]{1,0:T(8,128)(2,1)S(1)}, bf16[192,384]{1,0:T(8,128)(2,1)S(1)}, u32[]{:S(2)}, u32[]{:S(2)}) collective-permute-start(bf16[192,384]{1,0:T(8,128)(2,1)S(1)} %shard_map.95.refs_0_), channel_id=1, source_target_pairs={{0,48},{1,49},{2,50},{3,51},{4,52},{5,53},{6,54},{7,55},{8,56},{9,... | collective-permute-start | bytes 442376 | tf_op jit(solution)/shard_map/ppermute | solution.py:282
  43.0 0.0 collective-permute-done.1.refs_2_
  43.0 2.5 %collective-permute-start.6 = (bf16[192,384]{1,0:T(8,128)(2,1)S(1)}, bf16[192,384]{1,0:T(8,128)(2,1)S(1)}, u32[]{:S(2)}, u32[]{:S(2)}) collective-permute-start(bf16[192,384]{1,0:T(8,128)(2,1)S(1)} %shard_map.95.refs_0_), channel_id=1, source_target_pairs={{0,56},{1,57},{2,58},{3,59},{4,60},{5,61},{6,62},{7,63},{8,0},{9,1... | collective-permute-start | bytes 442376 | tf_op jit(solution)/shard_map/ppermute | solution.py:282
  45.5 7.7 %shard_map.96.weight_hbm = bf16[1024,3584]{1,0:T(8,128)(2,1)} custom-call(bf16[1024,3584]{1,0:T(8,128)(2,1)} %bitcast.28, s32[112,1024]{1,0:T(8,128)} %bitcast.30), custom_call_target="tpu_custom_call" | custom-call | flops 939524096 | bytes 14680064 | tf_op jit(solution)/shard_map/pallas_call | solution.py:284
  53.2 0.0 collective-permute-done.2.refs_3_
  53.3 0.0 collective-permute-done.3.refs_4_
  53.3 0.0 collective-permute-done.4.refs_5_
  53.3 0.0 collective-permute-done.5.refs_6_
  53.3 0.0 collective-permute-done.6.refs_7_
  53.3 0.0 all-to-all-done
  53.3 0.0 copy-start
  53.3 2.5 %shard_map.98 = bf16[8,672,128]{2,1,0:T(8,128)(2,1)} custom-call(s32[1]{0:T(128)} %bitcast.13.parity_ref, bf16[384,1792]{1,0:T(8,128)(2,1)S(1)} %bitcast.20), custom_call_target="tpu_custom_call" | custom-call | flops 704643072 | bytes 2752512 | tf_op jit(solution)/shard_map/pallas_call | solution.py:299
  55.8 0.0 copy-done
  55.8 7.2 %all-to-all-start.1 = ((bf16[8,672,128]{2,1,0:T(8,128)(2,1)}), bf16[8,672,128]{2,1,0:T(8,128)(2,1)S(1)}, u32[]{:S(2)}, u32[]{:S(2)}) async-start(bf16[8,672,128]{2,1,0:T(8,128)(2,1)} %shard_map.98), calls=%async_computation.1 | async-start | bytes 2752512 | tf_op jit(solution)/shard_map/all_to_all | solution.py:242
  63.0 6.2 %shard_map.97 = (bf16[192,1024]{1,0:T(8,128)(2,1)}, f32[8,128]{1,0:T(8,128)}, f32[8,128]{1,0:T(8,128)}) custom-call(s32[1]{0:T(128)} %bitcast.me_ref, bf16[384,1792]{1,0:T(8,128)(2,1)} %bitcast.21, bf16[1024,3584]{1,0:T(8,128)(2,1)} %shard_map.96.weight_hbm, bf16[192,1024]{1,0:T(8,128)(2,1)} %bitcast.26), custom_call_target="tpu_custom_call" | custom-call | flops 2818572288 | bytes 7340032 | tf_op jit(solution)/shard_map/pallas_call | solution.py:310
  69.3 1.0 collective-permute-start.7
  70.3 2.2 %collective-permute-done.7.refs_1_ = f32[8,128]{1,0:T(8,128)S(1)} collective-permute-done((f32[8,128]{1,0:T(8,128)}, f32[8,128]{1,0:T(8,128)S(1)}, u32[]{:S(2)}, u32[]{:S(2)}) %collective-permute-start.7) | collective-permute-done | bytes 4128 | tf_op jit(solution)/shard_map/ppermute | solution.py:247
  72.5 0.0 copy-start.1
  72.6 0.7 copy-done.1
  73.2 3.4 %collective-permute-start.8 = (f32[8,128]{1,0:T(8,128)S(1)}, f32[8,128]{1,0:T(8,128)S(1)}, u32[]{:S(2)}, u32[]{:S(2)}) collective-permute-start(f32[8,128]{1,0:T(8,128)S(1)} %get-tuple-element.37), channel_id=1, source_target_pairs={{0,128},{64,192},{128,256},{192,320},{256,384},{320,448},{384,512}... | collective-permute-start | bytes 12296 | tf_op jit(solution)/shard_map/ppermute | solution.py:247
  76.7 2.1 %collective-permute-done.8.refs_1_ = f32[8,128]{1,0:T(8,128)S(1)} collective-permute-done((f32[8,128]{1,0:T(8,128)S(1)}, f32[8,128]{1,0:T(8,128)S(1)}, u32[]{:S(2)}, u32[]{:S(2)}) %collective-permute-start.8) | collective-permute-done | bytes 4128 | tf_op jit(solution)/shard_map/ppermute | solution.py:247
  78.8 6.7 %all-to-all-done.1.relayed_ref = bf16[8,672,128]{2,1,0:T(8,128)(2,1)S(1)} async-done(((bf16[8,672,128]{2,1,0:T(8,128)(2,1)}), bf16[8,672,128]{2,1,0:T(8,128)(2,1)S(1)}, u32[]{:S(2)}, u32[]{:S(2)}) %all-to-all-start.1) | async-done | bytes 1376288 | tf_op jit(solution)/shard_map/all_to_all | solution.py:242
  85.5 5.5 %collective-permute-start.9 = (f32[8,128]{1,0:T(8,128)S(1)}, f32[8,128]{1,0:T(8,128)S(1)}, u32[]{:S(2)}, u32[]{:S(2)}) collective-permute-start(f32[8,128]{1,0:T(8,128)S(1)} %get-tuple-element.49), channel_id=1, source_target_pairs={{0,256},{64,320},{128,384},{192,448},{256,512},{320,576},{384,640}... | collective-permute-start | bytes 12296 | tf_op jit(solution)/shard_map/ppermute | solution.py:247
  91.0 0.0 copy-start.2
  91.0 0.0 copy-start.3
  91.0 2.3 %shard_map.101 = bf16[448,384]{1,0:T(8,128)(2,1)} custom-call(s32[1]{0:T(128)} %bitcast.12.me_ref, bf16[8,672,128]{2,1,0:T(8,128)(2,1)S(1)} %all-to-all-done.1.relayed_ref, bf16[192,384]{1,0:T(8,128)(2,1)S(1)} %shard_map.95.refs_0_, bf16[192,384]{1,0:T(8,128)(2,1)S(1)} %collective-permute-done.refs_1_, bf16[192,384]{1,0:T(8,128)(2,1)S(1)} %collective-permute-done.1.refs_2_, ...), custom_call_target="tpu_custom_call" | custom-call | flops 528482304 | bytes 2555904 | tf_op jit(solution)/shard_map/pallas_call | solution.py:345
  93.4 0.0 collective-permute-done.9.refs_1_
  93.4 9.8 %all-to-all-start.2 = ((bf16[8,56,384]{2,1,0:T(8,128)(2,1)}), bf16[8,56,384]{2,1,0:T(8,128)(2,1)S(1)}, u32[]{:S(2)}, u32[]{:S(2)}) async-start(bf16[8,56,384]{2,1,0:T(8,128)(2,1)} %bitcast.14), calls=%async_computation.2 | async-start | bytes 688128 | tf_op jit(solution)/shard_map/all_to_all | solution.py:242
  103.2 4.0 %collective-permute-start.10 = (f32[8,128]{1,0:T(8,128)S(1)}, f32[8,128]{1,0:T(8,128)S(1)}, u32[]{:S(2)}, u32[]{:S(2)}) collective-permute-start(f32[8,128]{1,0:T(8,128)S(1)} %get-tuple-element.54), channel_id=1, source_target_pairs={{0,512},{64,576},{128,640},{192,704},{256,768},{320,832},{384,896}... | collective-permute-start | bytes 12296 | tf_op jit(solution)/shard_map/ppermute | solution.py:247
  107.3 5.4 %collective-permute-done.10.refs_1_ = f32[8,128]{1,0:T(8,128)S(1)} collective-permute-done((f32[8,128]{1,0:T(8,128)S(1)}, f32[8,128]{1,0:T(8,128)S(1)}, u32[]{:S(2)}, u32[]{:S(2)}) %collective-permute-start.10) | collective-permute-done | bytes 4128 | tf_op jit(solution)/shard_map/ppermute | solution.py:247
  112.6 0.0 copy-done.2
  112.6 0.0 copy-done.3
  112.6 0.8 shard_map.103
  113.4 1.1 all-to-all-done.2
  114.6 0.7 convert_reduce_fusion
  (3 shorter events, 0.0 us)
Async XLA Ops:
  3.7 16.8 %copy-start.4 = (bf16[1,1,16,12,1024]{4,2,3,1,0:T(8,128)(2,1)S(1)}, bf16[1,1,16,12,1024]{4,2,3,1,0:T(8,128)(2,1)}, u32[]{:S(2)}) copy-start(bf16[1,1,16,12,1024]{4,2,3,1,0:T(8,128)(2,1)} %param.10) | copy-start | bytes 1179652
  3.7 16.8 %copy-start.5 = (s32[1,384]{1,0:T(1,128)S(1)}, s32[1,384]{1,0:T(1,128)}, u32[]{:S(2)}) copy-start(s32[1,384]{1,0:T(1,128)} %ids_ref) | copy-start | bytes 4612
  3.7 49.6 %all-to-all-start = ((bf16[16,24,1792]{2,1,0:T(8,128)(2,1)}), bf16[16,24,1792]{2,1,0:T(8,128)(2,1)S(1)}, u32[]{:S(2)}, u32[]{:S(2)}) async-start(bf16[16,24,1792]{2,1,0:T(8,128)(2,1)} %bitcast.29), calls=%async_computation | async-start | bytes 2752512 | tf_op jit(solution)/shard_map/all_to_all | solution.py:269
  20.9 16.1 %collective-permute-start = (bf16[192,384]{1,0:T(8,128)(2,1)S(1)}, bf16[192,384]{1,0:T(8,128)(2,1)S(1)}, u32[]{:S(2)}, u32[]{:S(2)}) collective-permute-start(bf16[192,384]{1,0:T(8,128)(2,1)S(1)} %shard_map.95.refs_0_), channel_id=1, source_target_pairs={{0,8},{1,9},{2,10},{3,11},{4,12},{5,13},{6,14},{7,15},{8,16},{9,17... | collective-permute-start | bytes 442376 | tf_op jit(solution)/shard_map/ppermute | solution.py:282
  22.8 20.2 %collective-permute-start.1 = (bf16[192,384]{1,0:T(8,128)(2,1)S(1)}, bf16[192,384]{1,0:T(8,128)(2,1)S(1)}, u32[]{:S(2)}, u32[]{:S(2)}) collective-permute-start(bf16[192,384]{1,0:T(8,128)(2,1)S(1)} %shard_map.95.refs_0_), channel_id=1, source_target_pairs={{0,16},{1,17},{2,18},{3,19},{4,20},{5,21},{6,22},{7,23},{8,24},{9,... | collective-permute-start | bytes 442376 | tf_op jit(solution)/shard_map/ppermute | solution.py:282
  24.7 28.5 %collective-permute-start.2 = (bf16[192,384]{1,0:T(8,128)(2,1)S(1)}, bf16[192,384]{1,0:T(8,128)(2,1)S(1)}, u32[]{:S(2)}, u32[]{:S(2)}) collective-permute-start(bf16[192,384]{1,0:T(8,128)(2,1)S(1)} %shard_map.95.refs_0_), channel_id=1, source_target_pairs={{0,24},{1,25},{2,26},{3,27},{4,28},{5,29},{6,30},{7,31},{8,32},{9,... | collective-permute-start | bytes 442376 | tf_op jit(solution)/shard_map/ppermute | solution.py:282
  26.6 26.6 %collective-permute-start.3 = (bf16[192,384]{1,0:T(8,128)(2,1)S(1)}, bf16[192,384]{1,0:T(8,128)(2,1)S(1)}, u32[]{:S(2)}, u32[]{:S(2)}) collective-permute-start(bf16[192,384]{1,0:T(8,128)(2,1)S(1)} %shard_map.95.refs_0_), channel_id=1, source_target_pairs={{0,32},{1,33},{2,34},{3,35},{4,36},{5,37},{6,38},{7,39},{8,40},{9,... | collective-permute-start | bytes 442376 | tf_op jit(solution)/shard_map/ppermute | solution.py:282
  35.0 18.2 %collective-permute-start.4 = (bf16[192,384]{1,0:T(8,128)(2,1)S(1)}, bf16[192,384]{1,0:T(8,128)(2,1)S(1)}, u32[]{:S(2)}, u32[]{:S(2)}) collective-permute-start(bf16[192,384]{1,0:T(8,128)(2,1)S(1)} %shard_map.95.refs_0_), channel_id=1, source_target_pairs={{0,40},{1,41},{2,42},{3,43},{4,44},{5,45},{6,46},{7,47},{8,48},{9,... | collective-permute-start | bytes 442376 | tf_op jit(solution)/shard_map/ppermute | solution.py:282
  37.0 16.3 %collective-permute-start.5 = (bf16[192,384]{1,0:T(8,128)(2,1)S(1)}, bf16[192,384]{1,0:T(8,128)(2,1)S(1)}, u32[]{:S(2)}, u32[]{:S(2)}) collective-permute-start(bf16[192,384]{1,0:T(8,128)(2,1)S(1)} %shard_map.95.refs_0_), channel_id=1, source_target_pairs={{0,48},{1,49},{2,50},{3,51},{4,52},{5,53},{6,54},{7,55},{8,56},{9,... | collective-permute-start | bytes 442376 | tf_op jit(solution)/shard_map/ppermute | solution.py:282
  43.0 10.3 %collective-permute-start.6 = (bf16[192,384]{1,0:T(8,128)(2,1)S(1)}, bf16[192,384]{1,0:T(8,128)(2,1)S(1)}, u32[]{:S(2)}, u32[]{:S(2)}) collective-permute-start(bf16[192,384]{1,0:T(8,128)(2,1)S(1)} %shard_map.95.refs_0_), channel_id=1, source_target_pairs={{0,56},{1,57},{2,58},{3,59},{4,60},{5,61},{6,62},{7,63},{8,0},{9,1... | collective-permute-start | bytes 442376 | tf_op jit(solution)/shard_map/ppermute | solution.py:282
  53.3 2.6 %copy-start = (bf16[16,24,1792]{2,1,0:T(8,128)(2,1)}, bf16[16,24,1792]{2,1,0:T(8,128)(2,1)S(1)}, u32[]{:S(2)}) copy-start(bf16[16,24,1792]{2,1,0:T(8,128)(2,1)S(1)} %all-to-all-done) | copy-start | bytes 4128772
  55.8 29.7 %all-to-all-start.1 = ((bf16[8,672,128]{2,1,0:T(8,128)(2,1)}), bf16[8,672,128]{2,1,0:T(8,128)(2,1)S(1)}, u32[]{:S(2)}, u32[]{:S(2)}) async-start(bf16[8,672,128]{2,1,0:T(8,128)(2,1)} %shard_map.98), calls=%async_computation.1 | async-start | bytes 2752512 | tf_op jit(solution)/shard_map/all_to_all | solution.py:242
  69.3 3.3 %collective-permute-start.7 = (f32[8,128]{1,0:T(8,128)}, f32[8,128]{1,0:T(8,128)S(1)}, u32[]{:S(2)}, u32[]{:S(2)}) collective-permute-start(f32[8,128]{1,0:T(8,128)} %get-tuple-element.35), channel_id=1, source_target_pairs={{0,64},{64,128},{128,192},{192,256},{256,320},{320,384},{384,448},... | collective-permute-start | bytes 12296 | tf_op jit(solution)/shard_map/ppermute | solution.py:247
  72.5 0.7 copy-start.1
  73.2 5.5 %collective-permute-start.8 = (f32[8,128]{1,0:T(8,128)S(1)}, f32[8,128]{1,0:T(8,128)S(1)}, u32[]{:S(2)}, u32[]{:S(2)}) collective-permute-start(f32[8,128]{1,0:T(8,128)S(1)} %get-tuple-element.37), channel_id=1, source_target_pairs={{0,128},{64,192},{128,256},{192,320},{256,384},{320,448},{384,512}... | collective-permute-start | bytes 12296 | tf_op jit(solution)/shard_map/ppermute | solution.py:247
  85.5 7.9 %collective-permute-start.9 = (f32[8,128]{1,0:T(8,128)S(1)}, f32[8,128]{1,0:T(8,128)S(1)}, u32[]{:S(2)}, u32[]{:S(2)}) collective-permute-start(f32[8,128]{1,0:T(8,128)S(1)} %get-tuple-element.49), channel_id=1, source_target_pairs={{0,256},{64,320},{128,384},{192,448},{256,512},{320,576},{384,640}... | collective-permute-start | bytes 12296 | tf_op jit(solution)/shard_map/ppermute | solution.py:247
  91.0 21.6 %copy-start.2 = (s32[128,1]{0,1:T(1,128)S(1)}, s32[128,1]{0,1:T(1,128)}, u32[]{:S(2)}) copy-start(s32[128,1]{0,1:T(1,128)} %param.9) | copy-start | bytes 1540
  91.0 21.6 %copy-start.3 = (bf16[128,1]{0,1:T(2,128)(2,1)S(1)}, bf16[128,1]{0,1:T(2,128)(2,1)}, u32[]{:S(2)}) copy-start(bf16[128,1]{0,1:T(2,128)(2,1)} %param.8) | copy-start | bytes 772
  93.4 21.2 %all-to-all-start.2 = ((bf16[8,56,384]{2,1,0:T(8,128)(2,1)}), bf16[8,56,384]{2,1,0:T(8,128)(2,1)S(1)}, u32[]{:S(2)}, u32[]{:S(2)}) async-start(bf16[8,56,384]{2,1,0:T(8,128)(2,1)} %bitcast.14), calls=%async_computation.2 | async-start | bytes 688128 | tf_op jit(solution)/shard_map/all_to_all | solution.py:242
  103.2 9.4 %collective-permute-start.10 = (f32[8,128]{1,0:T(8,128)S(1)}, f32[8,128]{1,0:T(8,128)S(1)}, u32[]{:S(2)}, u32[]{:S(2)}) collective-permute-start(f32[8,128]{1,0:T(8,128)S(1)} %get-tuple-element.54), channel_id=1, source_target_pairs={{0,512},{64,576},{128,640},{192,704},{256,768},{320,832},{384,896}... | collective-permute-start | bytes 12296 | tf_op jit(solution)/shard_map/ppermute | solution.py:247

commit v3 on v2

--- a/solution.py
+++ b/solution.py
@@ -340,7 +340,6 @@
 
     scores = regrouped(0, passed_on(0, scores))
     scores = regrouped(1, passed_on(1, scores))
-    relayed, scores = lax.optimization_barrier((relayed, scores))
     scores = passed_on(2, scores)
     summed = pl.pallas_call(
         functools.partial(partial_kernel, side),

time: 116 us -> 112 us (0.966)
  the two profiles are of different devices: /device:TPU:4 before, /device:TPU:20 now
where the time goes in v3:
time: 112 us; the launch traced here: 111 us
  starting transfers between devices  74.2 us (66%)
  Pallas kernels  23.1 us (21%)
  waiting for transfers between devices  11.7 us (10%)
    ppermute x7, starting transfers between devices, per_device(): others = [lax.ppermute(picked, BOTH, moves(by)) for by in range(1, side)]  33.7 us
    all_to_all x2, starting transfers between devices, exchange(): lax.all_to_all(x, BOTH, split_axis=0, concat_axis=0, tiled=True, axis_ind...  17.6 us
    ppermute x4, starting transfers between devices, shifted(): lax.ppermute(x, 'expert', [(e, (e + by) % experts_n) for e in range(exper...  15.5 us
    ppermute x4, waiting for transfers between devices, shifted(): lax.ppermute(x, 'expert', [(e, (e + by) % experts_n) for e in range(exper...  10.6 us
    pallas_call x1, Pallas kernels, per_device(): pl.pallas_call(weight_kernel, grid=(blocks,), out_shape=jax.ShapeDtypeStr...  7.73 us
    all_to_all x1, starting transfers between devices, per_device(): lax.all_to_all(packed.reshape(experts_n, 2 * slots, half), 'expert', spli...  7.42 us
    pallas_call x1, Pallas kernels, per_device(): pl.pallas_call(functools.partial(hidden_kernel, slots, sources), out_shap...  6.24 us
    pallas_call x1, Pallas kernels, per_device(): pl.pallas_call(functools.partial(pack_kernel, slots, experts_n), grid=(ch...  3.03 us
  transfers between devices with their start and end apart: 14, of which 4 were waited for; matrix products, arithmetic and copies ran while one was open for 0% of the time, Pallas kernels for 16%

profile of v3, /device:TPU:20, one launch (start us, length us, event | category | flops | bytes accessed | tf_op | source)
XLA Modules:
  0.0 111.3 jit_solution(17994574775659792695)
XLA Ops:
  0.6 3.0 %shard_map.94 = bf16[384,1792]{1,0:T(8,128)(2,1)} custom-call(s32[1,128]{1,0:T(1,128)} %bitcast.22, bf16[1,128]{1,0:T(2,128)(2,1)} %bitcast.24, bf16[128,3584]{1,0:T(8,128)(2,1)} %right_ref.1, bf16[128,3584]{1,0:T(8,128)(2,1)} %right_ref.1), custom_call_target="tpu_custom_call" | custom-call | flops 352321536 | bytes 2064384 | tf_op jit(solution)/shard_map/pallas_call | solution.py:255
  3.7 0.0 copy-start.4
  3.7 0.0 copy-start.5
  3.7 7.4 %all-to-all-start = ((bf16[16,24,1792]{2,1,0:T(8,128)(2,1)}), bf16[16,24,1792]{2,1,0:T(8,128)(2,1)S(1)}, u32[]{:S(2)}, u32[]{:S(2)}) async-start(bf16[16,24,1792]{2,1,0:T(8,128)(2,1)} %bitcast.29), calls=%async_computation | async-start | bytes 2752512 | tf_op jit(solution)/shard_map/all_to_all | solution.py:269
  11.1 0.0 copy-done.4
  11.1 0.0 copy-done.5
  11.1 0.4 shard_map.95.refs_0_
  11.5 3.6 %collective-permute-start = (bf16[192,384]{1,0:T(8,128)(2,1)S(1)}, bf16[192,384]{1,0:T(8,128)(2,1)S(1)}, u32[]{:S(2)}, u32[]{:S(2)}) collective-permute-start(bf16[192,384]{1,0:T(8,128)(2,1)S(1)} %shard_map.95.refs_0_), channel_id=1, source_target_pairs={{0,8},{1,9},{2,10},{3,11},{4,12},{5,13},{6,14},{7,15},{8,16},{9,17... | collective-permute-start | bytes 442376 | tf_op jit(solution)/shard_map/ppermute | solution.py:282
  15.1 5.9 %collective-permute-start.1 = (bf16[192,384]{1,0:T(8,128)(2,1)S(1)}, bf16[192,384]{1,0:T(8,128)(2,1)S(1)}, u32[]{:S(2)}, u32[]{:S(2)}) collective-permute-start(bf16[192,384]{1,0:T(8,128)(2,1)S(1)} %shard_map.95.refs_0_), channel_id=1, source_target_pairs={{0,16},{1,17},{2,18},{3,19},{4,20},{5,21},{6,22},{7,23},{8,24},{9,... | collective-permute-start | bytes 442376 | tf_op jit(solution)/shard_map/ppermute | solution.py:282
  21.0 3.2 %collective-permute-start.2 = (bf16[192,384]{1,0:T(8,128)(2,1)S(1)}, bf16[192,384]{1,0:T(8,128)(2,1)S(1)}, u32[]{:S(2)}, u32[]{:S(2)}) collective-permute-start(bf16[192,384]{1,0:T(8,128)(2,1)S(1)} %shard_map.95.refs_0_), channel_id=1, source_target_pairs={{0,24},{1,25},{2,26},{3,27},{4,28},{5,29},{6,30},{7,31},{8,32},{9,... | collective-permute-start | bytes 442376 | tf_op jit(solution)/shard_map/ppermute | solution.py:282
  24.2 9.7 %collective-permute-start.3 = (bf16[192,384]{1,0:T(8,128)(2,1)S(1)}, bf16[192,384]{1,0:T(8,128)(2,1)S(1)}, u32[]{:S(2)}, u32[]{:S(2)}) collective-permute-start(bf16[192,384]{1,0:T(8,128)(2,1)S(1)} %shard_map.95.refs_0_), channel_id=1, source_target_pairs={{0,32},{1,33},{2,34},{3,35},{4,36},{5,37},{6,38},{7,39},{8,40},{9,... | collective-permute-start | bytes 442376 | tf_op jit(solution)/shard_map/ppermute | solution.py:282
  33.9 6.9 %collective-permute-start.4 = (bf16[192,384]{1,0:T(8,128)(2,1)S(1)}, bf16[192,384]{1,0:T(8,128)(2,1)S(1)}, u32[]{:S(2)}, u32[]{:S(2)}) collective-permute-start(bf16[192,384]{1,0:T(8,128)(2,1)S(1)} %shard_map.95.refs_0_), channel_id=1, source_target_pairs={{0,40},{1,41},{2,42},{3,43},{4,44},{5,45},{6,46},{7,47},{8,48},{9,... | collective-permute-start | bytes 442376 | tf_op jit(solution)/shard_map/ppermute | solution.py:282
  40.8 0.0 collective-permute-done.refs_1_
  40.9 1.9 %collective-permute-start.5 = (bf16[192,384]{1,0:T(8,128)(2,1)S(1)}, bf16[192,384]{1,0:T(8,128)(2,1)S(1)}, u32[]{:S(2)}, u32[]{:S(2)}) collective-permute-start(bf16[192,384]{1,0:T(8,128)(2,1)S(1)} %shard_map.95.refs_0_), channel_id=1, source_target_pairs={{0,48},{1,49},{2,50},{3,51},{4,52},{5,53},{6,54},{7,55},{8,56},{9,... | collective-permute-start | bytes 442376 | tf_op jit(solution)/shard_map/ppermute | solution.py:282
  42.8 0.0 collective-permute-done.1.refs_2_
  42.8 2.5 %collective-permute-start.6 = (bf16[192,384]{1,0:T(8,128)(2,1)S(1)}, bf16[192,384]{1,0:T(8,128)(2,1)S(1)}, u32[]{:S(2)}, u32[]{:S(2)}) collective-permute-start(bf16[192,384]{1,0:T(8,128)(2,1)S(1)} %shard_map.95.refs_0_), channel_id=1, source_target_pairs={{0,56},{1,57},{2,58},{3,59},{4,60},{5,61},{6,62},{7,63},{8,0},{9,1... | collective-permute-start | bytes 442376 | tf_op jit(solution)/shard_map/ppermute | solution.py:282
  45.3 7.7 %shard_map.96.weight_hbm = bf16[1024,3584]{1,0:T(8,128)(2,1)} custom-call(bf16[1024,3584]{1,0:T(8,128)(2,1)} %bitcast.28, s32[112,1024]{1,0:T(8,128)} %bitcast.30), custom_call_target="tpu_custom_call" | custom-call | flops 939524096 | bytes 14680064 | tf_op jit(solution)/shard_map/pallas_call | solution.py:284
  53.0 0.0 collective-permute-done.2.refs_3_
  53.0 0.0 collective-permute-done.3.refs_4_
  53.0 0.0 collective-permute-done.4.refs_5_
  53.0 0.0 collective-permute-done.5.refs_6_
  53.1 0.0 collective-permute-done.6.refs_7_
  53.1 0.0 all-to-all-done
  53.1 0.0 copy-start
  53.1 2.5 %shard_map.98 = bf16[8,672,128]{2,1,0:T(8,128)(2,1)} custom-call(s32[1]{0:T(128)} %bitcast.13.parity_ref, bf16[384,1792]{1,0:T(8,128)(2,1)S(1)} %bitcast.20), custom_call_target="tpu_custom_call" | custom-call | flops 704643072 | bytes 2752512 | tf_op jit(solution)/shard_map/pallas_call | solution.py:299
  55.6 0.0 copy-done
  55.6 7.7 %all-to-all-start.1 = ((bf16[8,672,128]{2,1,0:T(8,128)(2,1)}), bf16[8,672,128]{2,1,0:T(8,128)(2,1)S(1)}, u32[]{:S(2)}, u32[]{:S(2)}) async-start(bf16[8,672,128]{2,1,0:T(8,128)(2,1)} %shard_map.98), calls=%async_computation.1 | async-start | bytes 2752512 | tf_op jit(solution)/shard_map/all_to_all | solution.py:242
  63.4 6.2 %shard_map.97 = (bf16[192,1024]{1,0:T(8,128)(2,1)}, f32[8,128]{1,0:T(8,128)}, f32[8,128]{1,0:T(8,128)}) custom-call(s32[1]{0:T(128)} %bitcast.me_ref, bf16[384,1792]{1,0:T(8,128)(2,1)} %bitcast.21, bf16[1024,3584]{1,0:T(8,128)(2,1)} %shard_map.96.weight_hbm, bf16[192,1024]{1,0:T(8,128)(2,1)} %bitcast.26), custom_call_target="tpu_custom_call" | custom-call | flops 2818572288 | bytes 7340032 | tf_op jit(solution)/shard_map/pallas_call | solution.py:310
  69.6 0.7 collective-permute-start.7
  70.3 2.6 %collective-permute-done.7.refs_1_ = f32[8,128]{1,0:T(8,128)S(1)} collective-permute-done((f32[8,128]{1,0:T(8,128)}, f32[8,128]{1,0:T(8,128)S(1)}, u32[]{:S(2)}, u32[]{:S(2)}) %collective-permute-start.7) | collective-permute-done | bytes 4128 | tf_op jit(solution)/shard_map/ppermute | solution.py:247
  72.9 0.0 copy-start.1
  72.9 0.7 copy-done.1
  73.6 3.4 %collective-permute-start.8 = (f32[8,128]{1,0:T(8,128)S(1)}, f32[8,128]{1,0:T(8,128)S(1)}, u32[]{:S(2)}, u32[]{:S(2)}) collective-permute-start(f32[8,128]{1,0:T(8,128)S(1)} %get-tuple-element.41), channel_id=1, source_target_pairs={{0,128},{64,192},{128,256},{192,320},{256,384},{320,448},{384,512}... | collective-permute-start | bytes 12296 | tf_op jit(solution)/shard_map/ppermute | solution.py:247
  77.0 2.1 %collective-permute-done.8.refs_1_ = f32[8,128]{1,0:T(8,128)S(1)} collective-permute-done((f32[8,128]{1,0:T(8,128)S(1)}, f32[8,128]{1,0:T(8,128)S(1)}, u32[]{:S(2)}, u32[]{:S(2)}) %collective-permute-start.8) | collective-permute-done | bytes 4128 | tf_op jit(solution)/shard_map/ppermute | solution.py:247
  79.1 7.9 %collective-permute-start.9 = (f32[8,128]{1,0:T(8,128)S(1)}, f32[8,128]{1,0:T(8,128)S(1)}, u32[]{:S(2)}, u32[]{:S(2)}) collective-permute-start(f32[8,128]{1,0:T(8,128)S(1)} %get-tuple-element.43), channel_id=1, source_target_pairs={{0,256},{64,320},{128,384},{192,448},{256,512},{320,576},{384,640}... | collective-permute-start | bytes 12296 | tf_op jit(solution)/shard_map/ppermute | solution.py:247
  87.0 0.0 all-to-all-done.1.relayed_ref
  87.0 0.0 copy-start.2
  87.0 0.0 copy-start.3
  87.1 2.3 %shard_map.99 = bf16[448,384]{1,0:T(8,128)(2,1)} custom-call(s32[1]{0:T(128)} %bitcast.12.me_ref, bf16[8,672,128]{2,1,0:T(8,128)(2,1)S(1)} %all-to-all-done.1.relayed_ref, bf16[192,384]{1,0:T(8,128)(2,1)S(1)} %shard_map.95.refs_0_, bf16[192,384]{1,0:T(8,128)(2,1)S(1)} %collective-permute-done.refs_1_, bf16[192,384]{1,0:T(8,128)(2,1)S(1)} %collective-permute-done.1.refs_2_, ...), custom_call_target="tpu_custom_call" | custom-call | flops 528482304 | bytes 2555904 | tf_op jit(solution)/shard_map/pallas_call | solution.py:344
  89.4 0.0 collective-permute-done.9.refs_1_
  89.4 9.8 %all-to-all-start.2 = ((bf16[8,56,384]{2,1,0:T(8,128)(2,1)}), bf16[8,56,384]{2,1,0:T(8,128)(2,1)S(1)}, u32[]{:S(2)}, u32[]{:S(2)}) async-start(bf16[8,56,384]{2,1,0:T(8,128)(2,1)} %bitcast.14), calls=%async_computation.2 | async-start | bytes 688128 | tf_op jit(solution)/shard_map/all_to_all | solution.py:242
  99.2 3.5 %collective-permute-start.10 = (f32[8,128]{1,0:T(8,128)S(1)}, f32[8,128]{1,0:T(8,128)S(1)}, u32[]{:S(2)}, u32[]{:S(2)}) collective-permute-start(f32[8,128]{1,0:T(8,128)S(1)} %get-tuple-element.48), channel_id=1, source_target_pairs={{0,512},{64,576},{128,640},{192,704},{256,768},{320,832},{384,896}... | collective-permute-start | bytes 12296 | tf_op jit(solution)/shard_map/ppermute | solution.py:247
  102.7 5.9 %collective-permute-done.10.refs_1_ = f32[8,128]{1,0:T(8,128)S(1)} collective-permute-done((f32[8,128]{1,0:T(8,128)S(1)}, f32[8,128]{1,0:T(8,128)S(1)}, u32[]{:S(2)}, u32[]{:S(2)}) %collective-permute-start.10) | collective-permute-done | bytes 4128 | tf_op jit(solution)/shard_map/ppermute | solution.py:247
  108.6 0.0 copy-done.2
  108.6 0.0 copy-done.3
  108.6 0.8 shard_map.103
  109.4 1.1 %all-to-all-done.2 = bf16[8,56,384]{2,1,0:T(8,128)(2,1)S(1)} async-done(((bf16[8,56,384]{2,1,0:T(8,128)(2,1)}), bf16[8,56,384]{2,1,0:T(8,128)(2,1)S(1)}, u32[]{:S(2)}, u32[]{:S(2)}) %all-to-all-start.2) | async-done | bytes 344096 | tf_op jit(solution)/shard_map/all_to_all | solution.py:242
  110.6 0.7 convert_reduce_fusion
  (3 shorter events, 0.0 us)
Async XLA Ops:
  3.7 7.4 %copy-start.4 = (bf16[1,1,16,12,1024]{4,2,3,1,0:T(8,128)(2,1)S(1)}, bf16[1,1,16,12,1024]{4,2,3,1,0:T(8,128)(2,1)}, u32[]{:S(2)}) copy-start(bf16[1,1,16,12,1024]{4,2,3,1,0:T(8,128)(2,1)} %param.10) | copy-start | bytes 1179652
  3.7 7.4 %copy-start.5 = (s32[1,384]{1,0:T(1,128)S(1)}, s32[1,384]{1,0:T(1,128)}, u32[]{:S(2)}) copy-start(s32[1,384]{1,0:T(1,128)} %ids_ref) | copy-start | bytes 4612
  3.7 49.4 %all-to-all-start = ((bf16[16,24,1792]{2,1,0:T(8,128)(2,1)}), bf16[16,24,1792]{2,1,0:T(8,128)(2,1)S(1)}, u32[]{:S(2)}, u32[]{:S(2)}) async-start(bf16[16,24,1792]{2,1,0:T(8,128)(2,1)} %bitcast.29), calls=%async_computation | async-start | bytes 2752512 | tf_op jit(solution)/shard_map/all_to_all | solution.py:269
  11.5 29.4 %collective-permute-start = (bf16[192,384]{1,0:T(8,128)(2,1)S(1)}, bf16[192,384]{1,0:T(8,128)(2,1)S(1)}, u32[]{:S(2)}, u32[]{:S(2)}) collective-permute-start(bf16[192,384]{1,0:T(8,128)(2,1)S(1)} %shard_map.95.refs_0_), channel_id=1, source_target_pairs={{0,8},{1,9},{2,10},{3,11},{4,12},{5,13},{6,14},{7,15},{8,16},{9,17... | collective-permute-start | bytes 442376 | tf_op jit(solution)/shard_map/ppermute | solution.py:282
  15.1 27.7 %collective-permute-start.1 = (bf16[192,384]{1,0:T(8,128)(2,1)S(1)}, bf16[192,384]{1,0:T(8,128)(2,1)S(1)}, u32[]{:S(2)}, u32[]{:S(2)}) collective-permute-start(bf16[192,384]{1,0:T(8,128)(2,1)S(1)} %shard_map.95.refs_0_), channel_id=1, source_target_pairs={{0,16},{1,17},{2,18},{3,19},{4,20},{5,21},{6,22},{7,23},{8,24},{9,... | collective-permute-start | bytes 442376 | tf_op jit(solution)/shard_map/ppermute | solution.py:282
  21.0 32.0 %collective-permute-start.2 = (bf16[192,384]{1,0:T(8,128)(2,1)S(1)}, bf16[192,384]{1,0:T(8,128)(2,1)S(1)}, u32[]{:S(2)}, u32[]{:S(2)}) collective-permute-start(bf16[192,384]{1,0:T(8,128)(2,1)S(1)} %shard_map.95.refs_0_), channel_id=1, source_target_pairs={{0,24},{1,25},{2,26},{3,27},{4,28},{5,29},{6,30},{7,31},{8,32},{9,... | collective-permute-start | bytes 442376 | tf_op jit(solution)/shard_map/ppermute | solution.py:282
  24.2 28.8 %collective-permute-start.3 = (bf16[192,384]{1,0:T(8,128)(2,1)S(1)}, bf16[192,384]{1,0:T(8,128)(2,1)S(1)}, u32[]{:S(2)}, u32[]{:S(2)}) collective-permute-start(bf16[192,384]{1,0:T(8,128)(2,1)S(1)} %shard_map.95.refs_0_), channel_id=1, source_target_pairs={{0,32},{1,33},{2,34},{3,35},{4,36},{5,37},{6,38},{7,39},{8,40},{9,... | collective-permute-start | bytes 442376 | tf_op jit(solution)/shard_map/ppermute | solution.py:282
  33.9 19.1 %collective-permute-start.4 = (bf16[192,384]{1,0:T(8,128)(2,1)S(1)}, bf16[192,384]{1,0:T(8,128)(2,1)S(1)}, u32[]{:S(2)}, u32[]{:S(2)}) collective-permute-start(bf16[192,384]{1,0:T(8,128)(2,1)S(1)} %shard_map.95.refs_0_), channel_id=1, source_target_pairs={{0,40},{1,41},{2,42},{3,43},{4,44},{5,45},{6,46},{7,47},{8,48},{9,... | collective-permute-start | bytes 442376 | tf_op jit(solution)/shard_map/ppermute | solution.py:282
  40.9 12.2 %collective-permute-start.5 = (bf16[192,384]{1,0:T(8,128)(2,1)S(1)}, bf16[192,384]{1,0:T(8,128)(2,1)S(1)}, u32[]{:S(2)}, u32[]{:S(2)}) collective-permute-start(bf16[192,384]{1,0:T(8,128)(2,1)S(1)} %shard_map.95.refs_0_), channel_id=1, source_target_pairs={{0,48},{1,49},{2,50},{3,51},{4,52},{5,53},{6,54},{7,55},{8,56},{9,... | collective-permute-start | bytes 442376 | tf_op jit(solution)/shard_map/ppermute | solution.py:282
  42.8 10.3 %collective-permute-start.6 = (bf16[192,384]{1,0:T(8,128)(2,1)S(1)}, bf16[192,384]{1,0:T(8,128)(2,1)S(1)}, u32[]{:S(2)}, u32[]{:S(2)}) collective-permute-start(bf16[192,384]{1,0:T(8,128)(2,1)S(1)} %shard_map.95.refs_0_), channel_id=1, source_target_pairs={{0,56},{1,57},{2,58},{3,59},{4,60},{5,61},{6,62},{7,63},{8,0},{9,1... | collective-permute-start | bytes 442376 | tf_op jit(solution)/shard_map/ppermute | solution.py:282
  53.1 2.6 %copy-start = (bf16[16,24,1792]{2,1,0:T(8,128)(2,1)}, bf16[16,24,1792]{2,1,0:T(8,128)(2,1)S(1)}, u32[]{:S(2)}) copy-start(bf16[16,24,1792]{2,1,0:T(8,128)(2,1)S(1)} %all-to-all-done) | copy-start | bytes 4128772
  55.6 31.4 %all-to-all-start.1 = ((bf16[8,672,128]{2,1,0:T(8,128)(2,1)}), bf16[8,672,128]{2,1,0:T(8,128)(2,1)S(1)}, u32[]{:S(2)}, u32[]{:S(2)}) async-start(bf16[8,672,128]{2,1,0:T(8,128)(2,1)} %shard_map.98), calls=%async_computation.1 | async-start | bytes 2752512 | tf_op jit(solution)/shard_map/all_to_all | solution.py:242
  69.6 3.3 %collective-permute-start.7 = (f32[8,128]{1,0:T(8,128)}, f32[8,128]{1,0:T(8,128)S(1)}, u32[]{:S(2)}, u32[]{:S(2)}) collective-permute-start(f32[8,128]{1,0:T(8,128)} %get-tuple-element.39), channel_id=1, source_target_pairs={{0,64},{64,128},{128,192},{192,256},{256,320},{320,384},{384,448},... | collective-permute-start | bytes 12296 | tf_op jit(solution)/shard_map/ppermute | solution.py:247
  72.9 0.7 copy-start.1
  73.6 5.5 %collective-permute-start.8 = (f32[8,128]{1,0:T(8,128)S(1)}, f32[8,128]{1,0:T(8,128)S(1)}, u32[]{:S(2)}, u32[]{:S(2)}) collective-permute-start(f32[8,128]{1,0:T(8,128)S(1)} %get-tuple-element.41), channel_id=1, source_target_pairs={{0,128},{64,192},{128,256},{192,320},{256,384},{320,448},{384,512}... | collective-permute-start | bytes 12296 | tf_op jit(solution)/shard_map/ppermute | solution.py:247
  79.1 10.3 %collective-permute-start.9 = (f32[8,128]{1,0:T(8,128)S(1)}, f32[8,128]{1,0:T(8,128)S(1)}, u32[]{:S(2)}, u32[]{:S(2)}) collective-permute-start(f32[8,128]{1,0:T(8,128)S(1)} %get-tuple-element.43), channel_id=1, source_target_pairs={{0,256},{64,320},{128,384},{192,448},{256,512},{320,576},{384,640}... | collective-permute-start | bytes 12296 | tf_op jit(solution)/shard_map/ppermute | solution.py:247
  87.0 21.6 %copy-start.2 = (s32[128,1]{0,1:T(1,128)S(1)}, s32[128,1]{0,1:T(1,128)}, u32[]{:S(2)}) copy-start(s32[128,1]{0,1:T(1,128)} %param.9) | copy-start | bytes 1540
  87.0 21.6 %copy-start.3 = (bf16[128,1]{0,1:T(2,128)(2,1)S(1)}, bf16[128,1]{0,1:T(2,128)(2,1)}, u32[]{:S(2)}) copy-start(bf16[128,1]{0,1:T(2,128)(2,1)} %param.8) | copy-start | bytes 772
  89.4 21.2 %all-to-all-start.2 = ((bf16[8,56,384]{2,1,0:T(8,128)(2,1)}), bf16[8,56,384]{2,1,0:T(8,128)(2,1)S(1)}, u32[]{:S(2)}, u32[]{:S(2)}) async-start(bf16[8,56,384]{2,1,0:T(8,128)(2,1)} %bitcast.14), calls=%async_computation.2 | async-start | bytes 688128 | tf_op jit(solution)/shard_map/all_to_all | solution.py:242
  99.2 9.4 %collective-permute-start.10 = (f32[8,128]{1,0:T(8,128)S(1)}, f32[8,128]{1,0:T(8,128)S(1)}, u32[]{:S(2)}, u32[]{:S(2)}) collective-permute-start(f32[8,128]{1,0:T(8,128)S(1)} %get-tuple-element.48), channel_id=1, source_target_pairs={{0,512},{64,576},{128,640},{192,704},{256,768},{320,832},{384,896}... | collective-permute-start | bytes 12296 | tf_op jit(solution)/shard_map/ppermute | solution.py:247

commit v4 on v3

--- a/solution.py
+++ b/solution.py
@@ -9,6 +9,7 @@
 
 F32 = jnp.float32
 BF16 = jnp.bfloat16
+F8 = jnp.float8_e5m2
 BOTH = ("expert", "replica")
 MIB = 1024 * 1024
 
@@ -104,7 +105,7 @@
 
     at = step_n * (block // 32) + (iota((groups, block), 1) >> 5)
     spread = contract(factors[...], ones_where(iota((groups, block), 0) == at), 1, 0)
-    out_ref[...] = codes_ref[...] * spread.astype(BF16)
+    out_ref[...] = (codes_ref[...] * spread.astype(BF16)).astype(out_ref.dtype)
 
 
 def hidden_kernel(slots, sources, me_ref, rows_hbm, weight_hbm, hidden_hbm, out_ref, *refs):
@@ -133,7 +134,7 @@
     for n, load in enumerate([first_load, *rest]):
         load.wait()
         part = slice(n * block, (n + 1) * block)
-        through = contract(rows[...], weight_ref[part, :], 1, 1)
+        through = contract(rows[...], weight_ref[part, :].astype(BF16), 1, 1)
         out_ref[:, part] = through.astype(BF16)
         score += jnp.sum(through * hidden_ref[:, part].astype(F32), axis=1, keepdims=True)
     by_slot = jnp.where(iota((places, 128), 1) == iota((places, 128), 0) >> 4, score, 0.0)
@@ -284,7 +285,7 @@
     weight = pl.pallas_call(
         weight_kernel,
         grid=(blocks,),
-        out_shape=jax.ShapeDtypeStruct((hidden_n, width), BF16),
+        out_shape=jax.ShapeDtypeStruct((hidden_n, width), F8),
         in_specs=[
             pl.BlockSpec((hidden_n, width // blocks), lambda i: (0, i)),
             pl.BlockSpec((width // 32, hidden_n), lambda i: (0, 0)),
@@ -317,7 +318,7 @@
         out_specs=(VMEM,) + (VMEM,) * radix,
         scratch_shapes=[
             pltpu.VMEM((2 * places, half), BF16),
-            pltpu.VMEM((hidden_n, width), BF16),
+            pltpu.VMEM((hidden_n, width), F8),
             pltpu.VMEM((places, hidden_n), BF16),
             pltpu.VMEM((places, width), BF16),
             pltpu.SemaphoreType.DMA((2 + 2,)),

time: 112 us -> 111 us (level)
  Pallas kernels: 23.1 us -> 21.7 us
  transfers between devices with their start and end apart: 14 -> 14, of which waited for: 4 -> 4; matrix products, arithmetic and copies ran while one was open for 0% -> 0% of each run, Pallas kernels for 16% -> 15%
where the time goes in v4:
time: 111 us; the launch traced here: 110 us
  starting transfers between devices  74.2 us (67%)
  Pallas kernels  21.7 us (20%)
  waiting for transfers between devices  11.8 us (11%)
    ppermute x7, starting transfers between devices, per_device(): others = [lax.ppermute(picked, BOTH, moves(by)) for by in range(1, side)]  33.7 us
    all_to_all x2, starting transfers between devices, exchange(): lax.all_to_all(x, BOTH, split_axis=0, concat_axis=0, tiled=True, axis_ind...  17.6 us
    ppermute x4, starting transfers between devices, shifted(): lax.ppermute(x, 'expert', [(e, (e + by) % experts_n) for e in range(exper...  15.5 us
    ppermute x4, waiting for transfers between devices, shifted(): lax.ppermute(x, 'expert', [(e, (e + by) % experts_n) for e in range(exper...  10.6 us
    all_to_all x1, starting transfers between devices, per_device(): lax.all_to_all(packed.reshape(experts_n, 2 * slots, half), 'expert', spli...  7.42 us
    pallas_call x1, Pallas kernels, per_device(): pl.pallas_call(weight_kernel, grid=(blocks,), out_shape=jax.ShapeDtypeStr...  6.8 us
    pallas_call x1, Pallas kernels, per_device(): pl.pallas_call(functools.partial(hidden_kernel, slots, sources), out_shap...  5.94 us
    pallas_call x1, Pallas kernels, per_device(): pl.pallas_call(functools.partial(pack_kernel, slots, experts_n), grid=(ch...  2.97 us
  transfers between devices with their start and end apart: 14, of which 4 were waited for; matrix products, arithmetic and copies ran while one was open for 0% of the time, Pallas kernels for 15%

profile of v4, /device:TPU:20, one launch (start us, length us, event | category | flops | bytes accessed | tf_op | source)
XLA Modules:
  0.0 109.9 jit_solution(6959702909858769628)
XLA Ops:
  0.6 3.0 %shard_map.94 = bf16[384,1792]{1,0:T(8,128)(2,1)} custom-call(s32[1,128]{1,0:T(1,128)} %bitcast.22, bf16[1,128]{1,0:T(2,128)(2,1)} %bitcast.24, bf16[128,3584]{1,0:T(8,128)(2,1)} %right_ref.1, bf16[128,3584]{1,0:T(8,128)(2,1)} %right_ref.1), custom_call_target="tpu_custom_call" | custom-call | flops 352321536 | bytes 2064384 | tf_op jit(solution)/shard_map/pallas_call | solution.py:256
  3.6 0.0 copy-start.4
  3.6 0.0 copy-start.5
  3.6 7.4 %all-to-all-start = ((bf16[16,24,1792]{2,1,0:T(8,128)(2,1)}), bf16[16,24,1792]{2,1,0:T(8,128)(2,1)S(1)}, u32[]{:S(2)}, u32[]{:S(2)}) async-start(bf16[16,24,1792]{2,1,0:T(8,128)(2,1)} %bitcast.29), calls=%async_computation | async-start | bytes 2752512 | tf_op jit(solution)/shard_map/all_to_all | solution.py:270
  11.0 0.0 copy-done.4
  11.0 0.0 copy-done.5
  11.0 0.4 shard_map.95.refs_0_
  11.4 3.6 %collective-permute-start = (bf16[192,384]{1,0:T(8,128)(2,1)S(1)}, bf16[192,384]{1,0:T(8,128)(2,1)S(1)}, u32[]{:S(2)}, u32[]{:S(2)}) collective-permute-start(bf16[192,384]{1,0:T(8,128)(2,1)S(1)} %shard_map.95.refs_0_), channel_id=1, source_target_pairs={{0,8},{1,9},{2,10},{3,11},{4,12},{5,13},{6,14},{7,15},{8,16},{9,17... | collective-permute-start | bytes 442376 | tf_op jit(solution)/shard_map/ppermute | solution.py:283
  15.0 5.9 %collective-permute-start.1 = (bf16[192,384]{1,0:T(8,128)(2,1)S(1)}, bf16[192,384]{1,0:T(8,128)(2,1)S(1)}, u32[]{:S(2)}, u32[]{:S(2)}) collective-permute-start(bf16[192,384]{1,0:T(8,128)(2,1)S(1)} %shard_map.95.refs_0_), channel_id=1, source_target_pairs={{0,16},{1,17},{2,18},{3,19},{4,20},{5,21},{6,22},{7,23},{8,24},{9,... | collective-permute-start | bytes 442376 | tf_op jit(solution)/shard_map/ppermute | solution.py:283
  21.0 3.2 %collective-permute-start.2 = (bf16[192,384]{1,0:T(8,128)(2,1)S(1)}, bf16[192,384]{1,0:T(8,128)(2,1)S(1)}, u32[]{:S(2)}, u32[]{:S(2)}) collective-permute-start(bf16[192,384]{1,0:T(8,128)(2,1)S(1)} %shard_map.95.refs_0_), channel_id=1, source_target_pairs={{0,24},{1,25},{2,26},{3,27},{4,28},{5,29},{6,30},{7,31},{8,32},{9,... | collective-permute-start | bytes 442376 | tf_op jit(solution)/shard_map/ppermute | solution.py:283
  24.1 9.7 %collective-permute-start.3 = (bf16[192,384]{1,0:T(8,128)(2,1)S(1)}, bf16[192,384]{1,0:T(8,128)(2,1)S(1)}, u32[]{:S(2)}, u32[]{:S(2)}) collective-permute-start(bf16[192,384]{1,0:T(8,128)(2,1)S(1)} %shard_map.95.refs_0_), channel_id=1, source_target_pairs={{0,32},{1,33},{2,34},{3,35},{4,36},{5,37},{6,38},{7,39},{8,40},{9,... | collective-permute-start | bytes 442376 | tf_op jit(solution)/shard_map/ppermute | solution.py:283
  33.9 6.9 %collective-permute-start.4 = (bf16[192,384]{1,0:T(8,128)(2,1)S(1)}, bf16[192,384]{1,0:T(8,128)(2,1)S(1)}, u32[]{:S(2)}, u32[]{:S(2)}) collective-permute-start(bf16[192,384]{1,0:T(8,128)(2,1)S(1)} %shard_map.95.refs_0_), channel_id=1, source_target_pairs={{0,40},{1,41},{2,42},{3,43},{4,44},{5,45},{6,46},{7,47},{8,48},{9,... | collective-permute-start | bytes 442376 | tf_op jit(solution)/shard_map/ppermute | solution.py:283
  40.8 0.0 collective-permute-done.refs_1_
  40.8 1.9 %collective-permute-start.5 = (bf16[192,384]{1,0:T(8,128)(2,1)S(1)}, bf16[192,384]{1,0:T(8,128)(2,1)S(1)}, u32[]{:S(2)}, u32[]{:S(2)}) collective-permute-start(bf16[192,384]{1,0:T(8,128)(2,1)S(1)} %shard_map.95.refs_0_), channel_id=1, source_target_pairs={{0,48},{1,49},{2,50},{3,51},{4,52},{5,53},{6,54},{7,55},{8,56},{9,... | collective-permute-start | bytes 442376 | tf_op jit(solution)/shard_map/ppermute | solution.py:283
  42.7 0.0 collective-permute-done.1.refs_2_
  42.7 2.5 %collective-permute-start.6 = (bf16[192,384]{1,0:T(8,128)(2,1)S(1)}, bf16[192,384]{1,0:T(8,128)(2,1)S(1)}, u32[]{:S(2)}, u32[]{:S(2)}) collective-permute-start(bf16[192,384]{1,0:T(8,128)(2,1)S(1)} %shard_map.95.refs_0_), channel_id=1, source_target_pairs={{0,56},{1,57},{2,58},{3,59},{4,60},{5,61},{6,62},{7,63},{8,0},{9,1... | collective-permute-start | bytes 442376 | tf_op jit(solution)/shard_map/ppermute | solution.py:283
  45.2 6.8 %shard_map.96.weight_hbm = f8e5m2[1024,3584]{1,0:T(32,128)(4,1)} custom-call(bf16[1024,3584]{1,0:T(8,128)(2,1)} %bitcast.28, s32[112,1024]{1,0:T(8,128)} %bitcast.30), custom_call_target="tpu_custom_call" | custom-call | flops 939524096 | bytes 14680064 | tf_op jit(solution)/shard_map/pallas_call | solution.py:285
  52.0 0.0 collective-permute-done.2.refs_3_
  52.0 0.0 collective-permute-done.3.refs_4_
  52.0 0.0 collective-permute-done.4.refs_5_
  52.1 0.0 collective-permute-done.5.refs_6_
  52.1 0.0 collective-permute-done.6.refs_7_
  52.1 0.0 all-to-all-done
  52.1 0.0 copy-start
  52.1 2.4 %shard_map.98 = bf16[8,672,128]{2,1,0:T(8,128)(2,1)} custom-call(s32[1]{0:T(128)} %bitcast.13.parity_ref, bf16[384,1792]{1,0:T(8,128)(2,1)S(1)} %bitcast.20), custom_call_target="tpu_custom_call" | custom-call | flops 704643072 | bytes 2752512 | tf_op jit(solution)/shard_map/pallas_call | solution.py:300
  54.5 0.0 copy-done
  54.5 7.8 %all-to-all-start.1 = ((bf16[8,672,128]{2,1,0:T(8,128)(2,1)}), bf16[8,672,128]{2,1,0:T(8,128)(2,1)S(1)}, u32[]{:S(2)}, u32[]{:S(2)}) async-start(bf16[8,672,128]{2,1,0:T(8,128)(2,1)} %shard_map.98), calls=%async_computation.1 | async-start | bytes 2752512 | tf_op jit(solution)/shard_map/all_to_all | solution.py:243
  62.3 5.9 %shard_map.97 = (bf16[192,1024]{1,0:T(8,128)(2,1)}, f32[8,128]{1,0:T(8,128)}, f32[8,128]{1,0:T(8,128)}) custom-call(s32[1]{0:T(128)} %bitcast.me_ref, bf16[384,1792]{1,0:T(8,128)(2,1)} %bitcast.21, f8e5m2[1024,3584]{1,0:T(32,128)(4,1)} %shard_map.96.weight_hbm, bf16[192,1024]{1,0:T(8,128)(2,1)} %bitcast.26), custom_call_target="tpu_custom_call" | custom-call | flops 2818572288 | bytes 7340032 | tf_op jit(solution)/shard_map/pallas_call | solution.py:311
  68.2 0.7 collective-permute-start.7
  68.9 2.6 %collective-permute-done.7.refs_1_ = f32[8,128]{1,0:T(8,128)S(1)} collective-permute-done((f32[8,128]{1,0:T(8,128)}, f32[8,128]{1,0:T(8,128)S(1)}, u32[]{:S(2)}, u32[]{:S(2)}) %collective-permute-start.7) | collective-permute-done | bytes 4128 | tf_op jit(solution)/shard_map/ppermute | solution.py:248
  71.5 0.0 copy-start.1
  71.5 0.7 copy-done.1
  72.2 3.4 %collective-permute-start.8 = (f32[8,128]{1,0:T(8,128)S(1)}, f32[8,128]{1,0:T(8,128)S(1)}, u32[]{:S(2)}, u32[]{:S(2)}) collective-permute-start(f32[8,128]{1,0:T(8,128)S(1)} %get-tuple-element.41), channel_id=1, source_target_pairs={{0,128},{64,192},{128,256},{192,320},{256,384},{320,448},{384,512}... | collective-permute-start | bytes 12296 | tf_op jit(solution)/shard_map/ppermute | solution.py:248
  75.6 2.1 %collective-permute-done.8.refs_1_ = f32[8,128]{1,0:T(8,128)S(1)} collective-permute-done((f32[8,128]{1,0:T(8,128)S(1)}, f32[8,128]{1,0:T(8,128)S(1)}, u32[]{:S(2)}, u32[]{:S(2)}) %collective-permute-start.8) | collective-permute-done | bytes 4128 | tf_op jit(solution)/shard_map/ppermute | solution.py:248
  77.7 7.9 %collective-permute-start.9 = (f32[8,128]{1,0:T(8,128)S(1)}, f32[8,128]{1,0:T(8,128)S(1)}, u32[]{:S(2)}, u32[]{:S(2)}) collective-permute-start(f32[8,128]{1,0:T(8,128)S(1)} %get-tuple-element.43), channel_id=1, source_target_pairs={{0,256},{64,320},{128,384},{192,448},{256,512},{320,576},{384,640}... | collective-permute-start | bytes 12296 | tf_op jit(solution)/shard_map/ppermute | solution.py:248
  85.6 0.0 all-to-all-done.1.relayed_ref
  85.7 0.0 copy-start.2
  85.7 0.0 copy-start.3
  85.7 2.3 %shard_map.99 = bf16[448,384]{1,0:T(8,128)(2,1)} custom-call(s32[1]{0:T(128)} %bitcast.12.me_ref, bf16[8,672,128]{2,1,0:T(8,128)(2,1)S(1)} %all-to-all-done.1.relayed_ref, bf16[192,384]{1,0:T(8,128)(2,1)S(1)} %shard_map.95.refs_0_, bf16[192,384]{1,0:T(8,128)(2,1)S(1)} %collective-permute-done.refs_1_, bf16[192,384]{1,0:T(8,128)(2,1)S(1)} %collective-permute-done.1.refs_2_, ...), custom_call_target="tpu_custom_call" | custom-call | flops 528482304 | bytes 2555904 | tf_op jit(solution)/shard_map/pallas_call | solution.py:345
  88.0 0.0 collective-permute-done.9.refs_1_
  88.0 9.8 %all-to-all-start.2 = ((bf16[8,56,384]{2,1,0:T(8,128)(2,1)}), bf16[8,56,384]{2,1,0:T(8,128)(2,1)S(1)}, u32[]{:S(2)}, u32[]{:S(2)}) async-start(bf16[8,56,384]{2,1,0:T(8,128)(2,1)} %bitcast.14), calls=%async_computation.2 | async-start | bytes 688128 | tf_op jit(solution)/shard_map/all_to_all | solution.py:243
  97.8 3.5 %collective-permute-start.10 = (f32[8,128]{1,0:T(8,128)S(1)}, f32[8,128]{1,0:T(8,128)S(1)}, u32[]{:S(2)}, u32[]{:S(2)}) collective-permute-start(f32[8,128]{1,0:T(8,128)S(1)} %get-tuple-element.48), channel_id=1, source_target_pairs={{0,512},{64,576},{128,640},{192,704},{256,768},{320,832},{384,896}... | collective-permute-start | bytes 12296 | tf_op jit(solution)/shard_map/ppermute | solution.py:248
  101.3 5.9 %collective-permute-done.10.refs_1_ = f32[8,128]{1,0:T(8,128)S(1)} collective-permute-done((f32[8,128]{1,0:T(8,128)S(1)}, f32[8,128]{1,0:T(8,128)S(1)}, u32[]{:S(2)}, u32[]{:S(2)}) %collective-permute-start.10) | collective-permute-done | bytes 4128 | tf_op jit(solution)/shard_map/ppermute | solution.py:248
  107.2 0.0 copy-done.2
  107.2 0.0 copy-done.3
  107.2 0.8 shard_map.103
  108.0 1.1 %all-to-all-done.2 = bf16[8,56,384]{2,1,0:T(8,128)(2,1)S(1)} async-done(((bf16[8,56,384]{2,1,0:T(8,128)(2,1)}), bf16[8,56,384]{2,1,0:T(8,128)(2,1)S(1)}, u32[]{:S(2)}, u32[]{:S(2)}) %all-to-all-start.2) | async-done | bytes 344096 | tf_op jit(solution)/shard_map/all_to_all | solution.py:243
  109.2 0.7 convert_reduce_fusion
  (3 shorter events, 0.0 us)
Async XLA Ops:
  3.6 7.4 %copy-start.4 = (bf16[1,1,16,12,1024]{4,2,3,1,0:T(8,128)(2,1)S(1)}, bf16[1,1,16,12,1024]{4,2,3,1,0:T(8,128)(2,1)}, u32[]{:S(2)}) copy-start(bf16[1,1,16,12,1024]{4,2,3,1,0:T(8,128)(2,1)} %param.10) | copy-start | bytes 1179652
  3.6 7.4 %copy-start.5 = (s32[1,384]{1,0:T(1,128)S(1)}, s32[1,384]{1,0:T(1,128)}, u32[]{:S(2)}) copy-start(s32[1,384]{1,0:T(1,128)} %ids_ref) | copy-start | bytes 4612
  3.6 48.5 %all-to-all-start = ((bf16[16,24,1792]{2,1,0:T(8,128)(2,1)}), bf16[16,24,1792]{2,1,0:T(8,128)(2,1)S(1)}, u32[]{:S(2)}, u32[]{:S(2)}) async-start(bf16[16,24,1792]{2,1,0:T(8,128)(2,1)} %bitcast.29), calls=%async_computation | async-start | bytes 2752512 | tf_op jit(solution)/shard_map/all_to_all | solution.py:270
  11.4 29.4 %collective-permute-start = (bf16[192,384]{1,0:T(8,128)(2,1)S(1)}, bf16[192,384]{1,0:T(8,128)(2,1)S(1)}, u32[]{:S(2)}, u32[]{:S(2)}) collective-permute-start(bf16[192,384]{1,0:T(8,128)(2,1)S(1)} %shard_map.95.refs_0_), channel_id=1, source_target_pairs={{0,8},{1,9},{2,10},{3,11},{4,12},{5,13},{6,14},{7,15},{8,16},{9,17... | collective-permute-start | bytes 442376 | tf_op jit(solution)/shard_map/ppermute | solution.py:283
  15.0 27.7 %collective-permute-start.1 = (bf16[192,384]{1,0:T(8,128)(2,1)S(1)}, bf16[192,384]{1,0:T(8,128)(2,1)S(1)}, u32[]{:S(2)}, u32[]{:S(2)}) collective-permute-start(bf16[192,384]{1,0:T(8,128)(2,1)S(1)} %shard_map.95.refs_0_), channel_id=1, source_target_pairs={{0,16},{1,17},{2,18},{3,19},{4,20},{5,21},{6,22},{7,23},{8,24},{9,... | collective-permute-start | bytes 442376 | tf_op jit(solution)/shard_map/ppermute | solution.py:283
  21.0 31.1 %collective-permute-start.2 = (bf16[192,384]{1,0:T(8,128)(2,1)S(1)}, bf16[192,384]{1,0:T(8,128)(2,1)S(1)}, u32[]{:S(2)}, u32[]{:S(2)}) collective-permute-start(bf16[192,384]{1,0:T(8,128)(2,1)S(1)} %shard_map.95.refs_0_), channel_id=1, source_target_pairs={{0,24},{1,25},{2,26},{3,27},{4,28},{5,29},{6,30},{7,31},{8,32},{9,... | collective-permute-start | bytes 442376 | tf_op jit(solution)/shard_map/ppermute | solution.py:283
  24.1 27.9 %collective-permute-start.3 = (bf16[192,384]{1,0:T(8,128)(2,1)S(1)}, bf16[192,384]{1,0:T(8,128)(2,1)S(1)}, u32[]{:S(2)}, u32[]{:S(2)}) collective-permute-start(bf16[192,384]{1,0:T(8,128)(2,1)S(1)} %shard_map.95.refs_0_), channel_id=1, source_target_pairs={{0,32},{1,33},{2,34},{3,35},{4,36},{5,37},{6,38},{7,39},{8,40},{9,... | collective-permute-start | bytes 442376 | tf_op jit(solution)/shard_map/ppermute | solution.py:283
  33.9 18.2 %collective-permute-start.4 = (bf16[192,384]{1,0:T(8,128)(2,1)S(1)}, bf16[192,384]{1,0:T(8,128)(2,1)S(1)}, u32[]{:S(2)}, u32[]{:S(2)}) collective-permute-start(bf16[192,384]{1,0:T(8,128)(2,1)S(1)} %shard_map.95.refs_0_), channel_id=1, source_target_pairs={{0,40},{1,41},{2,42},{3,43},{4,44},{5,45},{6,46},{7,47},{8,48},{9,... | collective-permute-start | bytes 442376 | tf_op jit(solution)/shard_map/ppermute | solution.py:283
  40.8 11.3 %collective-permute-start.5 = (bf16[192,384]{1,0:T(8,128)(2,1)S(1)}, bf16[192,384]{1,0:T(8,128)(2,1)S(1)}, u32[]{:S(2)}, u32[]{:S(2)}) collective-permute-start(bf16[192,384]{1,0:T(8,128)(2,1)S(1)} %shard_map.95.refs_0_), channel_id=1, source_target_pairs={{0,48},{1,49},{2,50},{3,51},{4,52},{5,53},{6,54},{7,55},{8,56},{9,... | collective-permute-start | bytes 442376 | tf_op jit(solution)/shard_map/ppermute | solution.py:283
  42.7 9.3 %collective-permute-start.6 = (bf16[192,384]{1,0:T(8,128)(2,1)S(1)}, bf16[192,384]{1,0:T(8,128)(2,1)S(1)}, u32[]{:S(2)}, u32[]{:S(2)}) collective-permute-start(bf16[192,384]{1,0:T(8,128)(2,1)S(1)} %shard_map.95.refs_0_), channel_id=1, source_target_pairs={{0,56},{1,57},{2,58},{3,59},{4,60},{5,61},{6,62},{7,63},{8,0},{9,1... | collective-permute-start | bytes 442376 | tf_op jit(solution)/shard_map/ppermute | solution.py:283
  52.1 2.4 %copy-start = (bf16[16,24,1792]{2,1,0:T(8,128)(2,1)}, bf16[16,24,1792]{2,1,0:T(8,128)(2,1)S(1)}, u32[]{:S(2)}) copy-start(bf16[16,24,1792]{2,1,0:T(8,128)(2,1)S(1)} %all-to-all-done) | copy-start | bytes 4128772
  54.5 31.1 %all-to-all-start.1 = ((bf16[8,672,128]{2,1,0:T(8,128)(2,1)}), bf16[8,672,128]{2,1,0:T(8,128)(2,1)S(1)}, u32[]{:S(2)}, u32[]{:S(2)}) async-start(bf16[8,672,128]{2,1,0:T(8,128)(2,1)} %shard_map.98), calls=%async_computation.1 | async-start | bytes 2752512 | tf_op jit(solution)/shard_map/all_to_all | solution.py:243
  68.2 3.3 %collective-permute-start.7 = (f32[8,128]{1,0:T(8,128)}, f32[8,128]{1,0:T(8,128)S(1)}, u32[]{:S(2)}, u32[]{:S(2)}) collective-permute-start(f32[8,128]{1,0:T(8,128)} %get-tuple-element.39), channel_id=1, source_target_pairs={{0,64},{64,128},{128,192},{192,256},{256,320},{320,384},{384,448},... | collective-permute-start | bytes 12296 | tf_op jit(solution)/shard_map/ppermute | solution.py:248
  71.5 0.7 copy-start.1
  72.2 5.5 %collective-permute-start.8 = (f32[8,128]{1,0:T(8,128)S(1)}, f32[8,128]{1,0:T(8,128)S(1)}, u32[]{:S(2)}, u32[]{:S(2)}) collective-permute-start(f32[8,128]{1,0:T(8,128)S(1)} %get-tuple-element.41), channel_id=1, source_target_pairs={{0,128},{64,192},{128,256},{192,320},{256,384},{320,448},{384,512}... | collective-permute-start | bytes 12296 | tf_op jit(solution)/shard_map/ppermute | solution.py:248
  77.7 10.3 %collective-permute-start.9 = (f32[8,128]{1,0:T(8,128)S(1)}, f32[8,128]{1,0:T(8,128)S(1)}, u32[]{:S(2)}, u32[]{:S(2)}) collective-permute-start(f32[8,128]{1,0:T(8,128)S(1)} %get-tuple-element.43), channel_id=1, source_target_pairs={{0,256},{64,320},{128,384},{192,448},{256,512},{320,576},{384,640}... | collective-permute-start | bytes 12296 | tf_op jit(solution)/shard_map/ppermute | solution.py:248
  85.7 21.6 %copy-start.2 = (s32[128,1]{0,1:T(1,128)S(1)}, s32[128,1]{0,1:T(1,128)}, u32[]{:S(2)}) copy-start(s32[128,1]{0,1:T(1,128)} %param.9) | copy-start | bytes 1540
  85.7 21.6 %copy-start.3 = (bf16[128,1]{0,1:T(2,128)(2,1)S(1)}, bf16[128,1]{0,1:T(2,128)(2,1)}, u32[]{:S(2)}) copy-start(bf16[128,1]{0,1:T(2,128)(2,1)} %param.8) | copy-start | bytes 772
  88.0 21.2 %all-to-all-start.2 = ((bf16[8,56,384]{2,1,0:T(8,128)(2,1)}), bf16[8,56,384]{2,1,0:T(8,128)(2,1)S(1)}, u32[]{:S(2)}, u32[]{:S(2)}) async-start(bf16[8,56,384]{2,1,0:T(8,128)(2,1)} %bitcast.14), calls=%async_computation.2 | async-start | bytes 688128 | tf_op jit(solution)/shard_map/all_to_all | solution.py:243
  97.8 9.4 %collective-permute-start.10 = (f32[8,128]{1,0:T(8,128)S(1)}, f32[8,128]{1,0:T(8,128)S(1)}, u32[]{:S(2)}, u32[]{:S(2)}) collective-permute-start(f32[8,128]{1,0:T(8,128)S(1)} %get-tuple-element.48), channel_id=1, source_target_pairs={{0,512},{64,576},{128,640},{192,704},{256,768},{320,832},{384,896}... | collective-permute-start | bytes 12296 | tf_op jit(solution)/shard_map/ppermute | solution.py:248

commit v5 on v4

--- a/solution.py
+++ b/solution.py
@@ -165,6 +165,10 @@
     out_ref[...] = total[...].astype(BF16)
 
 
+def keep_kernel(held_ref, out_ref):
+    out_ref[...] = held_ref[...]
+
+
 def with_bit(count, bit, value):
     return [j for j in range(count) if (j >> bit) & 1 == value]
 
@@ -339,7 +343,14 @@
             compiler_params=params,
         )(*scores)
 
-    scores = regrouped(0, passed_on(0, scores))
+    kept = pl.pallas_call(
+        keep_kernel,
+        out_shape=jax.ShapeDtypeStruct(scores[0].shape, F32),
+        in_specs=[VMEM],
+        out_specs=VMEM,
+        compiler_params=params,
+    )(scores[0])
+    scores = regrouped(0, [kept, shifted(scores[1], 1)])
     scores = regrouped(1, passed_on(1, scores))
     scores = passed_on(2, scores)
     summed = pl.pallas_call(

time: 111 us -> 110 us (level)
  no operation moved by 1% of the time
where the time goes in v5:
time: 110 us; the launch traced here: 109 us
  starting transfers between devices  74.5 us (68%)
  Pallas kernels  21.7 us (20%)
  waiting for transfers between devices  10.7 us (10%)
    ppermute x7, starting transfers between devices, per_device(): others = [lax.ppermute(picked, BOTH, moves(by)) for by in range(1, side)]  33.7 us
    all_to_all x2, starting transfers between devices, exchange(): lax.all_to_all(x, BOTH, split_axis=0, concat_axis=0, tiled=True, axis_ind...  17.6 us
    ppermute x4, starting transfers between devices, shifted(): lax.ppermute(x, 'expert', [(e, (e + by) % experts_n) for e in range(exper...  15.8 us
    ppermute x4, waiting for transfers between devices, shifted(): lax.ppermute(x, 'expert', [(e, (e + by) % experts_n) for e in range(exper...  9.58 us
    all_to_all x1, starting transfers between devices, per_device(): lax.all_to_all(packed.reshape(experts_n, 2 * slots, half), 'expert', spli...  7.42 us
    pallas_call x1, Pallas kernels, per_device(): pl.pallas_call(weight_kernel, grid=(blocks,), out_shape=jax.ShapeDtypeStr...  6.8 us
    pallas_call x1, Pallas kernels, per_device(): pl.pallas_call(functools.partial(hidden_kernel, slots, sources), out_shap...  5.94 us
    pallas_call x1, Pallas kernels, per_device(): pl.pallas_call(functools.partial(pack_kernel, slots, experts_n), grid=(ch...  2.97 us
  transfers between devices with their start and end apart: 14, of which 4 were waited for; matrix products, arithmetic and copies ran while one was open for 0% of the time, Pallas kernels for 15%

profile of v5, /device:TPU:20, one launch (start us, length us, event | category | flops | bytes accessed | tf_op | source)
XLA Modules:
  0.0 109.2 jit_solution(11435773394128948287)
XLA Ops:
  0.6 3.0 %shard_map.94 = bf16[384,1792]{1,0:T(8,128)(2,1)} custom-call(s32[1,128]{1,0:T(1,128)} %bitcast.22, bf16[1,128]{1,0:T(2,128)(2,1)} %bitcast.24, bf16[128,3584]{1,0:T(8,128)(2,1)} %right_ref.1, bf16[128,3584]{1,0:T(8,128)(2,1)} %right_ref.1), custom_call_target="tpu_custom_call" | custom-call | flops 352321536 | bytes 2064384 | tf_op jit(solution)/shard_map/pallas_call | solution.py:260
  3.6 0.0 copy-start.4
  3.6 0.0 copy-start.5
  3.6 7.4 %all-to-all-start = ((bf16[16,24,1792]{2,1,0:T(8,128)(2,1)}), bf16[16,24,1792]{2,1,0:T(8,128)(2,1)S(1)}, u32[]{:S(2)}, u32[]{:S(2)}) async-start(bf16[16,24,1792]{2,1,0:T(8,128)(2,1)} %bitcast.29), calls=%async_computation | async-start | bytes 2752512 | tf_op jit(solution)/shard_map/all_to_all | solution.py:274
  11.0 0.0 copy-done.4
  11.0 0.0 copy-done.5
  11.0 0.4 shard_map.95.refs_0_
  11.4 3.6 %collective-permute-start = (bf16[192,384]{1,0:T(8,128)(2,1)S(1)}, bf16[192,384]{1,0:T(8,128)(2,1)S(1)}, u32[]{:S(2)}, u32[]{:S(2)}) collective-permute-start(bf16[192,384]{1,0:T(8,128)(2,1)S(1)} %shard_map.95.refs_0_), channel_id=1, source_target_pairs={{0,8},{1,9},{2,10},{3,11},{4,12},{5,13},{6,14},{7,15},{8,16},{9,17... | collective-permute-start | bytes 442376 | tf_op jit(solution)/shard_map/ppermute | solution.py:287
  15.0 5.9 %collective-permute-start.1 = (bf16[192,384]{1,0:T(8,128)(2,1)S(1)}, bf16[192,384]{1,0:T(8,128)(2,1)S(1)}, u32[]{:S(2)}, u32[]{:S(2)}) collective-permute-start(bf16[192,384]{1,0:T(8,128)(2,1)S(1)} %shard_map.95.refs_0_), channel_id=1, source_target_pairs={{0,16},{1,17},{2,18},{3,19},{4,20},{5,21},{6,22},{7,23},{8,24},{9,... | collective-permute-start | bytes 442376 | tf_op jit(solution)/shard_map/ppermute | solution.py:287
  21.0 3.2 %collective-permute-start.2 = (bf16[192,384]{1,0:T(8,128)(2,1)S(1)}, bf16[192,384]{1,0:T(8,128)(2,1)S(1)}, u32[]{:S(2)}, u32[]{:S(2)}) collective-permute-start(bf16[192,384]{1,0:T(8,128)(2,1)S(1)} %shard_map.95.refs_0_), channel_id=1, source_target_pairs={{0,24},{1,25},{2,26},{3,27},{4,28},{5,29},{6,30},{7,31},{8,32},{9,... | collective-permute-start | bytes 442376 | tf_op jit(solution)/shard_map/ppermute | solution.py:287
  24.1 9.7 %collective-permute-start.3 = (bf16[192,384]{1,0:T(8,128)(2,1)S(1)}, bf16[192,384]{1,0:T(8,128)(2,1)S(1)}, u32[]{:S(2)}, u32[]{:S(2)}) collective-permute-start(bf16[192,384]{1,0:T(8,128)(2,1)S(1)} %shard_map.95.refs_0_), channel_id=1, source_target_pairs={{0,32},{1,33},{2,34},{3,35},{4,36},{5,37},{6,38},{7,39},{8,40},{9,... | collective-permute-start | bytes 442376 | tf_op jit(solution)/shard_map/ppermute | solution.py:287
  33.9 6.9 %collective-permute-start.4 = (bf16[192,384]{1,0:T(8,128)(2,1)S(1)}, bf16[192,384]{1,0:T(8,128)(2,1)S(1)}, u32[]{:S(2)}, u32[]{:S(2)}) collective-permute-start(bf16[192,384]{1,0:T(8,128)(2,1)S(1)} %shard_map.95.refs_0_), channel_id=1, source_target_pairs={{0,40},{1,41},{2,42},{3,43},{4,44},{5,45},{6,46},{7,47},{8,48},{9,... | collective-permute-start | bytes 442376 | tf_op jit(solution)/shard_map/ppermute | solution.py:287
  40.8 0.0 collective-permute-done.refs_1_
  40.8 1.9 %collective-permute-start.5 = (bf16[192,384]{1,0:T(8,128)(2,1)S(1)}, bf16[192,384]{1,0:T(8,128)(2,1)S(1)}, u32[]{:S(2)}, u32[]{:S(2)}) collective-permute-start(bf16[192,384]{1,0:T(8,128)(2,1)S(1)} %shard_map.95.refs_0_), channel_id=1, source_target_pairs={{0,48},{1,49},{2,50},{3,51},{4,52},{5,53},{6,54},{7,55},{8,56},{9,... | collective-permute-start | bytes 442376 | tf_op jit(solution)/shard_map/ppermute | solution.py:287
  42.7 0.0 collective-permute-done.1.refs_2_
  42.7 2.5 %collective-permute-start.6 = (bf16[192,384]{1,0:T(8,128)(2,1)S(1)}, bf16[192,384]{1,0:T(8,128)(2,1)S(1)}, u32[]{:S(2)}, u32[]{:S(2)}) collective-permute-start(bf16[192,384]{1,0:T(8,128)(2,1)S(1)} %shard_map.95.refs_0_), channel_id=1, source_target_pairs={{0,56},{1,57},{2,58},{3,59},{4,60},{5,61},{6,62},{7,63},{8,0},{9,1... | collective-permute-start | bytes 442376 | tf_op jit(solution)/shard_map/ppermute | solution.py:287
  45.2 6.8 %shard_map.96.weight_hbm = f8e5m2[1024,3584]{1,0:T(32,128)(4,1)} custom-call(bf16[1024,3584]{1,0:T(8,128)(2,1)} %bitcast.28, s32[112,1024]{1,0:T(8,128)} %bitcast.30), custom_call_target="tpu_custom_call" | custom-call | flops 939524096 | bytes 14680064 | tf_op jit(solution)/shard_map/pallas_call | solution.py:289
  52.0 0.0 collective-permute-done.2.refs_3_
  52.0 0.0 collective-permute-done.3.refs_4_
  52.0 0.0 collective-permute-done.4.refs_5_
  52.1 0.0 collective-permute-done.5.refs_6_
  52.1 0.0 collective-permute-done.6.refs_7_
  52.1 0.0 all-to-all-done
  52.1 0.0 copy-start
  52.1 2.4 %shard_map.98 = bf16[8,672,128]{2,1,0:T(8,128)(2,1)} custom-call(s32[1]{0:T(128)} %bitcast.13.parity_ref, bf16[384,1792]{1,0:T(8,128)(2,1)S(1)} %bitcast.20), custom_call_target="tpu_custom_call" | custom-call | flops 704643072 | bytes 2752512 | tf_op jit(solution)/shard_map/pallas_call | solution.py:304
  54.5 0.0 copy-done
  54.5 7.8 %all-to-all-start.1 = ((bf16[8,672,128]{2,1,0:T(8,128)(2,1)}), bf16[8,672,128]{2,1,0:T(8,128)(2,1)S(1)}, u32[]{:S(2)}, u32[]{:S(2)}) async-start(bf16[8,672,128]{2,1,0:T(8,128)(2,1)} %shard_map.98), calls=%async_computation.1 | async-start | bytes 2752512 | tf_op jit(solution)/shard_map/all_to_all | solution.py:247
  62.3 5.9 %shard_map.97 = (bf16[192,1024]{1,0:T(8,128)(2,1)}, f32[8,128]{1,0:T(8,128)}, f32[8,128]{1,0:T(8,128)}) custom-call(s32[1]{0:T(128)} %bitcast.me_ref, bf16[384,1792]{1,0:T(8,128)(2,1)} %bitcast.21, f8e5m2[1024,3584]{1,0:T(32,128)(4,1)} %shard_map.96.weight_hbm, bf16[192,1024]{1,0:T(8,128)(2,1)} %bitcast.26), custom_call_target="tpu_custom_call" | custom-call | flops 2818572288 | bytes 7340032 | tf_op jit(solution)/shard_map/pallas_call | solution.py:315
  68.2 0.7 collective-permute-start.7
  68.9 0.0 copy-start.1
  68.9 0.7 copy-done.1
  69.6 1.9 %collective-permute-done.7.refs_1_ = f32[8,128]{1,0:T(8,128)S(1)} collective-permute-done((f32[8,128]{1,0:T(8,128)}, f32[8,128]{1,0:T(8,128)S(1)}, u32[]{:S(2)}, u32[]{:S(2)}) %collective-permute-start.7) | collective-permute-done | bytes 4128 | tf_op jit(solution)/shard_map/ppermute | solution.py:252
  71.5 3.4 %collective-permute-start.8 = (f32[8,128]{1,0:T(8,128)S(1)}, f32[8,128]{1,0:T(8,128)S(1)}, u32[]{:S(2)}, u32[]{:S(2)}) collective-permute-start(f32[8,128]{1,0:T(8,128)S(1)} %get-tuple-element.41), channel_id=1, source_target_pairs={{0,128},{64,192},{128,256},{192,320},{256,384},{320,448},{384,512}... | collective-permute-start | bytes 12296 | tf_op jit(solution)/shard_map/ppermute | solution.py:252
  74.9 2.1 %collective-permute-done.8.refs_1_ = f32[8,128]{1,0:T(8,128)S(1)} collective-permute-done((f32[8,128]{1,0:T(8,128)S(1)}, f32[8,128]{1,0:T(8,128)S(1)}, u32[]{:S(2)}, u32[]{:S(2)}) %collective-permute-start.8) | collective-permute-done | bytes 4128 | tf_op jit(solution)/shard_map/ppermute | solution.py:252
  77.0 7.9 %collective-permute-start.9 = (f32[8,128]{1,0:T(8,128)S(1)}, f32[8,128]{1,0:T(8,128)S(1)}, u32[]{:S(2)}, u32[]{:S(2)}) collective-permute-start(f32[8,128]{1,0:T(8,128)S(1)} %get-tuple-element.43), channel_id=1, source_target_pairs={{0,256},{64,320},{128,384},{192,448},{256,512},{320,576},{384,640}... | collective-permute-start | bytes 12296 | tf_op jit(solution)/shard_map/ppermute | solution.py:252
  85.0 0.0 all-to-all-done.1.relayed_ref
  85.0 0.0 copy-start.2
  85.0 0.0 copy-start.3
  85.0 2.3 %shard_map.99 = bf16[448,384]{1,0:T(8,128)(2,1)} custom-call(s32[1]{0:T(128)} %bitcast.12.me_ref, bf16[8,672,128]{2,1,0:T(8,128)(2,1)S(1)} %all-to-all-done.1.relayed_ref, bf16[192,384]{1,0:T(8,128)(2,1)S(1)} %shard_map.95.refs_0_, bf16[192,384]{1,0:T(8,128)(2,1)S(1)} %collective-permute-done.refs_1_, bf16[192,384]{1,0:T(8,128)(2,1)S(1)} %collective-permute-done.1.refs_2_, ...), custom_call_target="tpu_custom_call" | custom-call | flops 528482304 | bytes 2555904 | tf_op jit(solution)/shard_map/pallas_call | solution.py:356
  87.3 0.0 collective-permute-done.9.refs_1_
  87.3 9.8 %all-to-all-start.2 = ((bf16[8,56,384]{2,1,0:T(8,128)(2,1)}), bf16[8,56,384]{2,1,0:T(8,128)(2,1)S(1)}, u32[]{:S(2)}, u32[]{:S(2)}) async-start(bf16[8,56,384]{2,1,0:T(8,128)(2,1)} %bitcast.14), calls=%async_computation.2 | async-start | bytes 688128 | tf_op jit(solution)/shard_map/all_to_all | solution.py:247
  97.2 3.8 %collective-permute-start.10 = (f32[8,128]{1,0:T(8,128)S(1)}, f32[8,128]{1,0:T(8,128)S(1)}, u32[]{:S(2)}, u32[]{:S(2)}) collective-permute-start(f32[8,128]{1,0:T(8,128)S(1)} %get-tuple-element.48), channel_id=1, source_target_pairs={{0,512},{64,576},{128,640},{192,704},{256,768},{320,832},{384,896}... | collective-permute-start | bytes 12296 | tf_op jit(solution)/shard_map/ppermute | solution.py:252
  101.0 5.6 %collective-permute-done.10.refs_1_ = f32[8,128]{1,0:T(8,128)S(1)} collective-permute-done((f32[8,128]{1,0:T(8,128)S(1)}, f32[8,128]{1,0:T(8,128)S(1)}, u32[]{:S(2)}, u32[]{:S(2)}) %collective-permute-start.10) | collective-permute-done | bytes 4128 | tf_op jit(solution)/shard_map/ppermute | solution.py:252
  106.6 0.0 copy-done.2
  106.6 0.0 copy-done.3
  106.6 0.8 shard_map.104
  107.4 1.1 %all-to-all-done.2 = bf16[8,56,384]{2,1,0:T(8,128)(2,1)S(1)} async-done(((bf16[8,56,384]{2,1,0:T(8,128)(2,1)}), bf16[8,56,384]{2,1,0:T(8,128)(2,1)S(1)}, u32[]{:S(2)}, u32[]{:S(2)}) %all-to-all-start.2) | async-done | bytes 344096 | tf_op jit(solution)/shard_map/all_to_all | solution.py:247
  108.5 0.7 convert_reduce_fusion
  (4 shorter events, 0.0 us)
Async XLA Ops:
  3.6 7.4 %copy-start.4 = (bf16[1,1,16,12,1024]{4,2,3,1,0:T(8,128)(2,1)S(1)}, bf16[1,1,16,12,1024]{4,2,3,1,0:T(8,128)(2,1)}, u32[]{:S(2)}) copy-start(bf16[1,1,16,12,1024]{4,2,3,1,0:T(8,128)(2,1)} %param.10) | copy-start | bytes 1179652
  3.6 7.4 %copy-start.5 = (s32[1,384]{1,0:T(1,128)S(1)}, s32[1,384]{1,0:T(1,128)}, u32[]{:S(2)}) copy-start(s32[1,384]{1,0:T(1,128)} %ids_ref) | copy-start | bytes 4612
  3.6 48.5 %all-to-all-start = ((bf16[16,24,1792]{2,1,0:T(8,128)(2,1)}), bf16[16,24,1792]{2,1,0:T(8,128)(2,1)S(1)}, u32[]{:S(2)}, u32[]{:S(2)}) async-start(bf16[16,24,1792]{2,1,0:T(8,128)(2,1)} %bitcast.29), calls=%async_computation | async-start | bytes 2752512 | tf_op jit(solution)/shard_map/all_to_all | solution.py:274
  11.4 29.4 %collective-permute-start = (bf16[192,384]{1,0:T(8,128)(2,1)S(1)}, bf16[192,384]{1,0:T(8,128)(2,1)S(1)}, u32[]{:S(2)}, u32[]{:S(2)}) collective-permute-start(bf16[192,384]{1,0:T(8,128)(2,1)S(1)} %shard_map.95.refs_0_), channel_id=1, source_target_pairs={{0,8},{1,9},{2,10},{3,11},{4,12},{5,13},{6,14},{7,15},{8,16},{9,17... | collective-permute-start | bytes 442376 | tf_op jit(solution)/shard_map/ppermute | solution.py:287
  15.0 27.7 %collective-permute-start.1 = (bf16[192,384]{1,0:T(8,128)(2,1)S(1)}, bf16[192,384]{1,0:T(8,128)(2,1)S(1)}, u32[]{:S(2)}, u32[]{:S(2)}) collective-permute-start(bf16[192,384]{1,0:T(8,128)(2,1)S(1)} %shard_map.95.refs_0_), channel_id=1, source_target_pairs={{0,16},{1,17},{2,18},{3,19},{4,20},{5,21},{6,22},{7,23},{8,24},{9,... | collective-permute-start | bytes 442376 | tf_op jit(solution)/shard_map/ppermute | solution.py:287
  21.0 31.1 %collective-permute-start.2 = (bf16[192,384]{1,0:T(8,128)(2,1)S(1)}, bf16[192,384]{1,0:T(8,128)(2,1)S(1)}, u32[]{:S(2)}, u32[]{:S(2)}) collective-permute-start(bf16[192,384]{1,0:T(8,128)(2,1)S(1)} %shard_map.95.refs_0_), channel_id=1, source_target_pairs={{0,24},{1,25},{2,26},{3,27},{4,28},{5,29},{6,30},{7,31},{8,32},{9,... | collective-permute-start | bytes 442376 | tf_op jit(solution)/shard_map/ppermute | solution.py:287
  24.1 27.9 %collective-permute-start.3 = (bf16[192,384]{1,0:T(8,128)(2,1)S(1)}, bf16[192,384]{1,0:T(8,128)(2,1)S(1)}, u32[]{:S(2)}, u32[]{:S(2)}) collective-permute-start(bf16[192,384]{1,0:T(8,128)(2,1)S(1)} %shard_map.95.refs_0_), channel_id=1, source_target_pairs={{0,32},{1,33},{2,34},{3,35},{4,36},{5,37},{6,38},{7,39},{8,40},{9,... | collective-permute-start | bytes 442376 | tf_op jit(solution)/shard_map/ppermute | solution.py:287
  33.9 18.2 %collective-permute-start.4 = (bf16[192,384]{1,0:T(8,128)(2,1)S(1)}, bf16[192,384]{1,0:T(8,128)(2,1)S(1)}, u32[]{:S(2)}, u32[]{:S(2)}) collective-permute-start(bf16[192,384]{1,0:T(8,128)(2,1)S(1)} %shard_map.95.refs_0_), channel_id=1, source_target_pairs={{0,40},{1,41},{2,42},{3,43},{4,44},{5,45},{6,46},{7,47},{8,48},{9,... | collective-permute-start | bytes 442376 | tf_op jit(solution)/shard_map/ppermute | solution.py:287
  40.8 11.3 %collective-permute-start.5 = (bf16[192,384]{1,0:T(8,128)(2,1)S(1)}, bf16[192,384]{1,0:T(8,128)(2,1)S(1)}, u32[]{:S(2)}, u32[]{:S(2)}) collective-permute-start(bf16[192,384]{1,0:T(8,128)(2,1)S(1)} %shard_map.95.refs_0_), channel_id=1, source_target_pairs={{0,48},{1,49},{2,50},{3,51},{4,52},{5,53},{6,54},{7,55},{8,56},{9,... | collective-permute-start | bytes 442376 | tf_op jit(solution)/shard_map/ppermute | solution.py:287
  42.7 9.3 %collective-permute-start.6 = (bf16[192,384]{1,0:T(8,128)(2,1)S(1)}, bf16[192,384]{1,0:T(8,128)(2,1)S(1)}, u32[]{:S(2)}, u32[]{:S(2)}) collective-permute-start(bf16[192,384]{1,0:T(8,128)(2,1)S(1)} %shard_map.95.refs_0_), channel_id=1, source_target_pairs={{0,56},{1,57},{2,58},{3,59},{4,60},{5,61},{6,62},{7,63},{8,0},{9,1... | collective-permute-start | bytes 442376 | tf_op jit(solution)/shard_map/ppermute | solution.py:287
  52.1 2.4 %copy-start = (bf16[16,24,1792]{2,1,0:T(8,128)(2,1)}, bf16[16,24,1792]{2,1,0:T(8,128)(2,1)S(1)}, u32[]{:S(2)}) copy-start(bf16[16,24,1792]{2,1,0:T(8,128)(2,1)S(1)} %all-to-all-done) | copy-start | bytes 4128772
  54.5 30.4 %all-to-all-start.1 = ((bf16[8,672,128]{2,1,0:T(8,128)(2,1)}), bf16[8,672,128]{2,1,0:T(8,128)(2,1)S(1)}, u32[]{:S(2)}, u32[]{:S(2)}) async-start(bf16[8,672,128]{2,1,0:T(8,128)(2,1)} %shard_map.98), calls=%async_computation.1 | async-start | bytes 2752512 | tf_op jit(solution)/shard_map/all_to_all | solution.py:247
  68.2 3.3 %collective-permute-start.7 = (f32[8,128]{1,0:T(8,128)}, f32[8,128]{1,0:T(8,128)S(1)}, u32[]{:S(2)}, u32[]{:S(2)}) collective-permute-start(f32[8,128]{1,0:T(8,128)} %get-tuple-element.39), channel_id=1, source_target_pairs={{0,64},{64,128},{128,192},{192,256},{256,320},{320,384},{384,448},... | collective-permute-start | bytes 12296 | tf_op jit(solution)/shard_map/ppermute | solution.py:252
  68.9 0.7 copy-start.1
  71.5 5.5 %collective-permute-start.8 = (f32[8,128]{1,0:T(8,128)S(1)}, f32[8,128]{1,0:T(8,128)S(1)}, u32[]{:S(2)}, u32[]{:S(2)}) collective-permute-start(f32[8,128]{1,0:T(8,128)S(1)} %get-tuple-element.41), channel_id=1, source_target_pairs={{0,128},{64,192},{128,256},{192,320},{256,384},{320,448},{384,512}... | collective-permute-start | bytes 12296 | tf_op jit(solution)/shard_map/ppermute | solution.py:252
  77.0 10.3 %collective-permute-start.9 = (f32[8,128]{1,0:T(8,128)S(1)}, f32[8,128]{1,0:T(8,128)S(1)}, u32[]{:S(2)}, u32[]{:S(2)}) collective-permute-start(f32[8,128]{1,0:T(8,128)S(1)} %get-tuple-element.43), channel_id=1, source_target_pairs={{0,256},{64,320},{128,384},{192,448},{256,512},{320,576},{384,640}... | collective-permute-start | bytes 12296 | tf_op jit(solution)/shard_map/ppermute | solution.py:252
  85.0 21.6 %copy-start.2 = (s32[128,1]{0,1:T(1,128)S(1)}, s32[128,1]{0,1:T(1,128)}, u32[]{:S(2)}) copy-start(s32[128,1]{0,1:T(1,128)} %param.9) | copy-start | bytes 1540
  85.0 21.6 %copy-start.3 = (bf16[128,1]{0,1:T(2,128)(2,1)S(1)}, bf16[128,1]{0,1:T(2,128)(2,1)}, u32[]{:S(2)}) copy-start(bf16[128,1]{0,1:T(2,128)(2,1)} %param.8) | copy-start | bytes 772
  87.3 21.2 %all-to-all-start.2 = ((bf16[8,56,384]{2,1,0:T(8,128)(2,1)}), bf16[8,56,384]{2,1,0:T(8,128)(2,1)S(1)}, u32[]{:S(2)}, u32[]{:S(2)}) async-start(bf16[8,56,384]{2,1,0:T(8,128)(2,1)} %bitcast.14), calls=%async_computation.2 | async-start | bytes 688128 | tf_op jit(solution)/shard_map/all_to_all | solution.py:247
  97.2 9.4 %collective-permute-start.10 = (f32[8,128]{1,0:T(8,128)S(1)}, f32[8,128]{1,0:T(8,128)S(1)}, u32[]{:S(2)}, u32[]{:S(2)}) collective-permute-start(f32[8,128]{1,0:T(8,128)S(1)} %get-tuple-element.48), channel_id=1, source_target_pairs={{0,512},{64,576},{128,640},{192,704},{256,768},{320,832},{384,896}... | collective-permute-start | bytes 12296 | tf_op jit(solution)/shard_map/ppermute | solution.py:252
